TPU v7x, 32 devices: a whole 2x2x4 slice. The times are simulated.
32 devices in a mesh: expert: 8 (over z, y), tensor: 4 (over x, core).
Axes of the slice: x: 2, y: 2, z: 4, core: 2. Of those that a mesh axis runs over, the one named last changes fastest.
Arguments:
- tokens: bfloat16 [4096, 2048], P('expert'), may hold values from -6 to 6
- segments: int32 [8, 512], P('expert'), may hold values from 0 to 2, never falling along the last dimension, each value on 1 to 256 neighbouring positions
- routes: int32 [4096, 6], P('expert'), may hold values from 0 to 15, all different within a row; in each aligned block of 512 rows (0 to 511, 512 to 1023, ...) at most 320 rows name the same one
- cotangent: bfloat16 [4096, 2048], P('expert'), may hold values from -6 to 6
- norm_in: bfloat16 [2048], P('expert'), may hold values from 0.5 to 1.5
- w_query: bfloat16 [2048, 3072], P('expert', 'tensor'), may hold values from -0.125 to 0.125
- w_latent: bfloat16 [2048, 576], P('expert'), may hold values from -0.125 to 0.125
- norm_latent: bfloat16 [512], P('expert'), may hold values from 0.5 to 1.5
- w_keyval: bfloat16 [512, 4096], P('expert', 'tensor'), may hold values from -0.25 to 0.25
- w_out: bfloat16 [2048, 2048], P('expert', 'tensor'), may hold values from -0.5 to 0.5
- norm_mid: bfloat16 [2048], P('expert'), may hold values from 0.5 to 1.5
- w_router: bfloat16 [2048, 16], P('expert'), may hold values from -0.0625 to 0.0625
- shared_gate: bfloat16 [2048, 2816], P('expert', 'tensor'), may hold values from -0.125 to 0.125
- shared_up: bfloat16 [2048, 2816], P('expert', 'tensor'), may hold values from -0.125 to 0.125
- shared_down: bfloat16 [2048, 2816], P('expert', 'tensor'), may hold values from -0.109375 to 0.109375
- expert_gate: bfloat16 [16, 2048, 1408], P('expert', None, 'tensor'), may hold values from -0.125 to 0.125
- expert_up: bfloat16 [16, 2048, 1408], P('expert', None, 'tensor'), may hold values from -0.125 to 0.125
- expert_down: bfloat16 [16, 1408, 2048], P('expert', 'tensor'), may hold values from -0.15625 to 0.15625
Outputs:
- mixed: bfloat16 [4096, 2048], P('expert', 'tensor')
- tokens_grad: bfloat16 [4096, 2048], P(('expert', 'tensor'))
- grad_norm_in: float32 [2048], P(('expert', 'tensor'))
- grad_w_query: float32 [2048, 3072], P('expert', 'tensor')
- grad_w_latent: float32 [2048, 576], P(('expert', 'tensor'))
- grad_norm_latent: float32 [512], P(('expert', 'tensor'))
- grad_w_keyval: float32 [512, 4096], P('expert', 'tensor')
- grad_w_out: float32 [2048, 2048], P('expert', 'tensor')
- grad_norm_mid: float32 [2048], P(('expert', 'tensor'))
- grad_w_router: float32 [2048, 16], P(('expert', 'tensor'))
- grad_shared_gate: float32 [2048, 2816], P('expert', 'tensor')
- grad_shared_up: float32 [2048, 2816], P('expert', 'tensor')
- grad_shared_down: float32 [2048, 2816], P('expert', 'tensor')
- grad_expert_gate: float32 [16, 2048, 1408], P('expert', None, 'tensor')
- grad_expert_up: float32 [16, 2048, 1408], P('expert', None, 'tensor')
- grad_expert_down: float32 [16, 1408, 2048], P('expert', 'tensor')
Inputs may be any that keep to these rules, and one draw needn't show every extreme that they name: `segments`: each row is one sequence of 512 tokens; document numbers never fall along it, each document has 1 to 256 tokens and one has exactly 256. `routes`: A token's 6 experts differ. In each aligned block of 512 rows (one sequence) no expert is named by more than 320 rows, a bound that some block reaches.
All inputs are finite; a program needn't handle non-finite values.
Results may differ from a plain program's by a relative error of at most 0.025.
Values may be sent and summed in bfloat16 or wider, within the bound.
A program may use at most 384 MiB of HBM per device.

v0:
```python
import jax
import jax.numpy as jnp
from jax import lax
from jax.sharding import PartitionSpec as P

D = 2048
NOPE = 128
ROPE = 64
VD = 128
KVR = 512
TOP = 6


EPS = 1e-06
ROUTE_SCALE = 2.446
THETA = 50000.0
NEG = -1e30
HIGH = lax.Precision.HIGHEST


def inv_rms(vec_in):
    return lax.rsqrt(jnp.mean(vec_in * vec_in, axis=-1, keepdims=True) + EPS)


def doc_positions(seg_ids):
    row_index = jnp.arange(seg_ids.shape[0], dtype=jnp.int32)
    starts = jnp.concatenate(
        [jnp.ones((1,), jnp.int32), (seg_ids[1:] != seg_ids[:-1]).astype(jnp.int32)]
    )
    first_idx = lax.cummax(jnp.where(starts > 0, row_index, jnp.zeros_like(row_index)), axis=0)
    return row_index - first_idx


def rope_tables(positions):
    half_dim = ROPE // 2
    freqs = THETA ** (-(jnp.arange(half_dim, dtype=jnp.float32) * 2.0 / ROPE))
    angles = positions.astype(jnp.float32)[:, None] * freqs[None, :]
    return (jnp.cos(angles), jnp.sin(angles))


def rotate(vec_in, cos_tab, sin_tab):
    half_dim = vec_in.shape[-1] // 2
    first_h = vec_in[..., :half_dim]
    second_h = vec_in[..., half_dim:]
    return jnp.concatenate(
        [first_h * cos_tab - second_h * sin_tab, first_h * sin_tab + second_h * cos_tab], axis=-1
    )


def unrotate(grad_in, cos_tab, sin_tab):
    half_dim = grad_in.shape[-1] // 2
    first_g = grad_in[..., :half_dim]
    second_g = grad_in[..., half_dim:]
    return jnp.concatenate(
        [first_g * cos_tab + second_g * sin_tab, second_g * cos_tab - first_g * sin_tab], axis=-1
    )


def dot_plain(left_m, right_m):
    return jnp.dot(left_m, right_m, preferred_element_type=jnp.float32)


def dot_last(left_m, right_m):
    return lax.dot_general(
        left_m, right_m, (((1,), (1,)), ((), ())), preferred_element_type=jnp.float32
    )


def dot_first(left_m, right_m):
    return lax.dot_general(
        left_m, right_m, (((0,), (0,)), ((), ())), preferred_element_type=jnp.float32
    )


def norm_back(field_in, inv_scale, gain_f, grad_in):
    scaled = grad_in * gain_f
    grad_field = inv_scale * scaled - field_in * inv_scale**3 * jnp.mean(
        field_in * scaled, axis=-1, keepdims=True
    )
    grad_gain = jnp.sum(grad_in * field_in * inv_scale, axis=0)
    return (grad_field, grad_gain)


def send_rows(rows_in):
    return lax.all_to_all(rows_in, "expert", split_axis=0, concat_axis=0, tiled=True)


def return_rows(rows_in):
    return lax.all_to_all(rows_in, "expert", split_axis=0, concat_axis=0, tiled=True)


def masked_scores(qn_blk, qr_blk, key_nope, key_rope, seg_blk, seg_ids, first_row):
    block_len = qn_blk.shape[0]
    scores = jnp.einsum("qhd,khd->hqk", qn_blk, key_nope, preferred_element_type=jnp.float32)
    scores = scores + jnp.einsum(
        "qhd,kd->hqk", qr_blk, key_rope, preferred_element_type=jnp.float32
    )
    scores = scores * (NOPE + ROPE) ** (-0.5)
    row_pos = first_row + jnp.arange(block_len, dtype=jnp.int32)
    col_pos = jnp.arange(key_nope.shape[0], dtype=jnp.int32)
    allowed = (seg_blk[:, None] == seg_ids[None, :]) & (row_pos[:, None] >= col_pos[None, :])
    return jnp.where(allowed[None], scores, NEG)


def local(
    tokens,
    segments,
    routes,
    cotangent,
    norm_in,
    w_query,
    w_latent,
    norm_latent,
    w_keyval,
    w_out,
    norm_mid,
    w_router,
    shared_gate,
    shared_up,
    shared_down,
    expert_gate,
    expert_up,
    expert_down,
):
    (
        gain_in,
        query_full,
        latent_full,
        gain_lat,
        keyval_full,
        outproj_full,
        gain_mid,
        router_full,
        shgate_full,
        shup_full,
        shdown_full,
    ) = (
        lax.all_gather(norm_in, "expert", axis=0, tiled=True),
        lax.all_gather(w_query, "expert", axis=0, tiled=True),
        lax.all_gather(w_latent, "expert", axis=0, tiled=True),
        lax.all_gather(norm_latent, "expert", axis=0, tiled=True),
        lax.all_gather(w_keyval, "expert", axis=0, tiled=True),
        lax.all_gather(w_out, "expert", axis=0, tiled=True),
        lax.all_gather(norm_mid, "expert", axis=0, tiled=True),
        lax.all_gather(w_router, "expert", axis=0, tiled=True),
        lax.all_gather(shared_gate, "expert", axis=0, tiled=True),
        lax.all_gather(shared_up, "expert", axis=0, tiled=True),
        lax.all_gather(shared_down, "expert", axis=0, tiled=True),
    )
    seq_len = tokens.shape[0]
    heads_local = query_full.shape[1] // (NOPE + ROPE)
    experts_all = router_full.shape[1]
    experts_here = expert_gate.shape[0]
    expert_count = lax.axis_size("expert")
    tensor_count = lax.axis_size("tensor")
    tensor_pos = lax.axis_index("tensor")
    capacity = 5 * seq_len * TOP // (3 * experts_all)
    quarter = D // tensor_count
    gain_in_f = gain_in.astype(jnp.float32)
    gain_lat_f = gain_lat.astype(jnp.float32)
    gain_mid_f = gain_mid.astype(jnp.float32)
    tok_f = tokens.astype(jnp.float32)
    inv_in = inv_rms(tok_f)
    normed = (tok_f * inv_in * gain_in_f).astype(jnp.bfloat16)
    query_lin = dot_plain(normed, query_full).reshape(seq_len, heads_local, NOPE + ROPE)
    seg_ids = segments[0]
    cos_tab, sin_tab = rope_tables(doc_positions(seg_ids))
    q_nope = query_lin[..., :NOPE].astype(jnp.bfloat16)
    q_rope = rotate(query_lin[..., NOPE:], cos_tab[:, None, :], sin_tab[:, None, :]).astype(
        jnp.bfloat16
    )
    latent_all = dot_plain(normed, latent_full)
    latent = latent_all[:, :KVR]
    inv_lat = inv_rms(latent)
    latent_n = (latent * inv_lat * gain_lat_f).astype(jnp.bfloat16)
    keyval = dot_plain(latent_n, keyval_full).reshape(seq_len, heads_local, NOPE + VD)
    key_nope = keyval[..., :NOPE].astype(jnp.bfloat16)
    values = keyval[..., NOPE:].astype(jnp.bfloat16)
    key_rope = rotate(latent_all[:, KVR:], cos_tab, sin_tab).astype(jnp.bfloat16)
    block_count = max(seq_len // 512, 1)
    block_len = seq_len // block_count

    def forward_block(block_no):
        start = block_no * block_len
        scores = masked_scores(q_nope, q_rope, key_nope, key_rope, seg_ids, seg_ids, start)
        top_val = jnp.max(scores, axis=-1, keepdims=True)
        expo = jnp.exp(scores - top_val)
        summed = jnp.sum(expo, axis=-1, keepdims=True)
        result = jnp.einsum(
            "hqk,khd->qhd",
            (expo / summed).astype(jnp.bfloat16),
            values,
            preferred_element_type=jnp.float32,
        )
        return (result.astype(jnp.bfloat16), top_val[..., 0] + jnp.log(summed[..., 0]))

    attended, log_norm = lax.map(forward_block, jnp.arange(block_count, dtype=jnp.int32))
    attended = attended.reshape(seq_len, heads_local * VD)
    attn_out = lax.psum(dot_last(attended, outproj_full).astype(jnp.bfloat16), "tensor").astype(
        jnp.float32
    )
    residual = tok_f + attn_out
    inv_mid = inv_rms(residual)
    normed_mid = (residual * inv_mid * gain_mid_f).astype(jnp.bfloat16)
    router_prob = jax.nn.sigmoid(dot_plain(normed_mid, router_full))
    expert_ids = jnp.arange(experts_all, dtype=jnp.int32)
    pick_mask = routes[:, :, None] == expert_ids[None, None, :]
    chosen = jnp.sum(jnp.where(pick_mask, router_prob[:, None, :], 0.0), axis=-1)
    chosen_sum = jnp.sum(chosen, axis=1, keepdims=True)
    gate_weights = ROUTE_SCALE * chosen / chosen_sum
    gate_sh = dot_plain(normed_mid, shgate_full)
    up_sh = dot_plain(normed_mid, shup_full)
    sig_sh = jax.nn.sigmoid(gate_sh)
    hidden_sh = (gate_sh * sig_sh * up_sh).astype(jnp.bfloat16)
    shared_out = dot_last(hidden_sh, shdown_full)
    flat_route = routes.reshape(-1)
    onehot = (flat_route[:, None] == expert_ids[None, :]).astype(jnp.int32)
    slot_no = jnp.sum(jnp.cumsum(onehot, axis=0) * onehot, axis=1) - 1
    dest_idx = flat_route * capacity + slot_no
    source_tok = (
        jnp.zeros((experts_all * capacity,), jnp.int32)
        .at[dest_idx]
        .set(jnp.arange(seq_len * TOP, dtype=jnp.int32) // TOP)
    )
    live_mask = jnp.zeros((experts_all * capacity,), jnp.bfloat16).at[dest_idx].set(1.0)
    outgoing = normed_mid[source_tok] * live_mask[:, None]
    outgoing = outgoing.reshape(expert_count, experts_here, capacity, outgoing.shape[1])
    arrived = send_rows(outgoing)
    gate_x = jnp.einsum("secd,edf->secf", arrived, expert_gate, preferred_element_type=jnp.float32)
    up_x = jnp.einsum("secd,edf->secf", arrived, expert_up, preferred_element_type=jnp.float32)
    sig_x = jax.nn.sigmoid(gate_x)
    hidden_x = (gate_x * sig_x * up_x).astype(jnp.bfloat16)
    out_x = jnp.einsum(
        "secf,efd->secd", hidden_x, expert_down, preferred_element_type=jnp.float32
    ).astype(jnp.bfloat16)
    returned = return_rows(out_x).reshape(experts_all * capacity, D)
    picked = returned[dest_idx].reshape(seq_len, TOP, D)
    routed = jnp.einsum("lk,lkd->ld", gate_weights, picked.astype(jnp.float32))
    moe_term = shared_out + routed
    moe_total = lax.psum_scatter(
        moe_term.astype(jnp.bfloat16), "tensor", scatter_dimension=1, tiled=True
    ).astype(jnp.float32)
    mixed = (
        lax.dynamic_slice_in_dim(residual, tensor_pos * quarter, quarter, 1) + moe_total
    ).astype(jnp.bfloat16)
    grad_out = cotangent.astype(jnp.float32)
    grad_hidden_sh = dot_plain(cotangent, shdown_full)
    grad_shdown = dot_first(cotangent, hidden_sh)
    grad_gate_sh = (grad_hidden_sh * up_sh * sig_sh * (1.0 + gate_sh * (1.0 - sig_sh))).astype(
        jnp.bfloat16
    )
    grad_up_sh = (grad_hidden_sh * gate_sh * sig_sh).astype(jnp.bfloat16)
    grad_shgate = dot_first(normed_mid, grad_gate_sh)
    grad_shup = dot_first(normed_mid, grad_up_sh)
    grad_mid = dot_last(grad_gate_sh, shgate_full) + dot_last(grad_up_sh, shup_full)
    gate_slots = (
        jnp.zeros((experts_all * capacity,), jnp.float32).at[dest_idx].set(gate_weights.reshape(-1))
    )
    grad_send = (grad_out[source_tok] * gate_slots[:, None]).astype(jnp.bfloat16)
    grad_send = grad_send.reshape(expert_count, experts_here, capacity, grad_send.shape[1])
    grad_arrived = send_rows(grad_send)
    grad_hidden_x = jnp.einsum(
        "secd,efd->secf", grad_arrived, expert_down, preferred_element_type=jnp.float32
    )
    grad_down_x = jnp.einsum(
        "secf,secd->efd", hidden_x, grad_arrived, preferred_element_type=jnp.float32
    )
    grad_gate_x = (grad_hidden_x * up_x * sig_x * (1.0 + gate_x * (1.0 - sig_x))).astype(
        jnp.bfloat16
    )
    grad_up_x = (grad_hidden_x * gate_x * sig_x).astype(jnp.bfloat16)
    grad_wgate_x = jnp.einsum(
        "secd,secf->edf", arrived, grad_gate_x, preferred_element_type=jnp.float32
    )
    grad_wup_x = jnp.einsum(
        "secd,secf->edf", arrived, grad_up_x, preferred_element_type=jnp.float32
    )
    grad_slots = jnp.einsum(
        "secf,edf->secd", grad_gate_x, expert_gate, preferred_element_type=jnp.float32
    )
    grad_slots = (
        grad_slots
        + jnp.einsum("secf,edf->secd", grad_up_x, expert_up, preferred_element_type=jnp.float32)
    ).astype(jnp.bfloat16)
    grad_home = return_rows(grad_slots).reshape(experts_all * capacity, D)
    grad_mid = grad_mid + jnp.sum(
        grad_home[dest_idx].reshape(seq_len, TOP, D).astype(jnp.float32), axis=1
    )
    grad_gates = jnp.einsum("ld,lkd->lk", cotangent, picked, preferred_element_type=jnp.float32)
    grad_chosen = (
        ROUTE_SCALE * grad_gates - jnp.sum(grad_gates * gate_weights, axis=1, keepdims=True)
    ) / chosen_sum
    grad_prob = jnp.sum(jnp.where(pick_mask, grad_chosen[:, :, None], 0.0), axis=1)
    grad_logit = grad_prob * router_prob * (1.0 - router_prob)
    router_f = router_full.astype(jnp.float32)
    grad_mid = grad_mid + jnp.dot(grad_logit, router_f.T, precision=HIGH)
    grad_router = jnp.dot(normed_mid.astype(jnp.float32).T, grad_logit, precision=HIGH)
    resid_part, grad_gain_mid = norm_back(residual, inv_mid, gain_mid_f, grad_mid)
    grad_resid = grad_out + lax.psum(resid_part.astype(jnp.bfloat16), "tensor").astype(jnp.float32)
    grad_attn = grad_resid.astype(jnp.bfloat16)
    grad_outproj = dot_first(grad_attn, attended)
    grad_att = (
        dot_plain(grad_attn, outproj_full).astype(jnp.bfloat16).reshape(seq_len, heads_local, VD)
    )
    score_scale = (NOPE + ROPE) ** (-0.5)

    def backward_block(carry, block_no):
        acc_knope, acc_krope, acc_values = carry
        start = block_no * block_len
        scores = masked_scores(q_nope, q_rope, key_nope, key_rope, seg_ids, seg_ids, start)
        probs_blk = jnp.exp(scores - log_norm[block_no][..., None])
        grad_probs = jnp.einsum(
            "qhd,khd->hqk", grad_att, values, preferred_element_type=jnp.float32
        )
        delta_sum = jnp.sum(probs_blk * grad_probs, axis=-1, keepdims=True)
        grad_scores = (probs_blk * (grad_probs - delta_sum)).astype(jnp.bfloat16)
        grad_qn = (
            jnp.einsum("hqk,khd->qhd", grad_scores, key_nope, preferred_element_type=jnp.float32)
            * score_scale
        )
        grad_qr = (
            jnp.einsum("hqk,kd->qhd", grad_scores, key_rope, preferred_element_type=jnp.float32)
            * score_scale
        )
        acc_knope = (
            acc_knope
            + jnp.einsum("hqk,qhd->khd", grad_scores, q_nope, preferred_element_type=jnp.float32)
            * score_scale
        )
        acc_krope = (
            acc_krope
            + jnp.einsum("hqk,qhd->kd", grad_scores, q_rope, preferred_element_type=jnp.float32)
            * score_scale
        )
        acc_values = acc_values + jnp.einsum(
            "hqk,qhd->khd",
            probs_blk.astype(jnp.bfloat16),
            grad_att,
            preferred_element_type=jnp.float32,
        )
        return ((acc_knope, acc_krope, acc_values), (grad_qn, grad_qr))

    start_acc = (
        jnp.zeros((seq_len, heads_local, NOPE), jnp.float32),
        jnp.zeros((seq_len, ROPE), jnp.float32),
        jnp.zeros((seq_len, heads_local, VD), jnp.float32),
    )
    (grad_knope, grad_krope, grad_values), (grad_qn, grad_qr) = lax.scan(
        backward_block, start_acc, jnp.arange(block_count, dtype=jnp.int32)
    )
    grad_qn = grad_qn.reshape(seq_len, heads_local, NOPE)
    grad_qr = unrotate(
        grad_qr.reshape(seq_len, heads_local, ROPE), cos_tab[:, None, :], sin_tab[:, None, :]
    )
    grad_query = (
        jnp.concatenate([grad_qn, grad_qr], axis=-1)
        .reshape(seq_len, heads_local * (NOPE + ROPE))
        .astype(jnp.bfloat16)
    )
    grad_wquery = dot_first(normed, grad_query)
    grad_normed = dot_last(grad_query, query_full)
    grad_keyval = (
        jnp.concatenate([grad_knope, grad_values], axis=-1)
        .reshape(seq_len, heads_local * (NOPE + VD))
        .astype(jnp.bfloat16)
    )
    grad_wkeyval = dot_first(latent_n, grad_keyval)
    grad_latent_n = dot_last(grad_keyval, keyval_full)
    grad_latent, grad_gain_lat = norm_back(latent, inv_lat, gain_lat_f, grad_latent_n)
    grad_latent_all = jnp.concatenate(
        [grad_latent, unrotate(grad_krope, cos_tab, sin_tab)], axis=-1
    )
    latent_f = latent_full.astype(jnp.float32)
    grad_normed = grad_normed + jnp.dot(grad_latent_all, latent_f.T, precision=HIGH)
    grad_wlatent = jnp.dot(normed.astype(jnp.float32).T, grad_latent_all, precision=HIGH)
    tok_part, grad_gain_in = norm_back(tok_f, inv_in, gain_in_f, grad_normed)
    (
        part_gain_in,
        out_wquery,
        part_wlatent,
        part_gain_lat,
        out_wkeyval,
        out_wout,
        part_gain_mid,
        part_router,
        out_shgate,
        out_shup,
        out_shdown,
    ) = (
        lax.psum_scatter(
            grad_gain_in.astype(jnp.bfloat16), "expert", scatter_dimension=0, tiled=True
        ).astype(jnp.float32),
        lax.psum_scatter(
            grad_wquery.astype(jnp.bfloat16), "expert", scatter_dimension=0, tiled=True
        ).astype(jnp.float32),
        lax.psum_scatter(
            grad_wlatent.astype(jnp.bfloat16), "expert", scatter_dimension=0, tiled=True
        ).astype(jnp.float32),
        lax.psum_scatter(
            grad_gain_lat.astype(jnp.bfloat16), "expert", scatter_dimension=0, tiled=True
        ).astype(jnp.float32),
        lax.psum_scatter(
            grad_wkeyval.astype(jnp.bfloat16), "expert", scatter_dimension=0, tiled=True
        ).astype(jnp.float32),
        lax.psum_scatter(
            grad_outproj.astype(jnp.bfloat16), "expert", scatter_dimension=0, tiled=True
        ).astype(jnp.float32),
        lax.psum_scatter(
            grad_gain_mid.astype(jnp.bfloat16), "expert", scatter_dimension=0, tiled=True
        ).astype(jnp.float32),
        lax.psum_scatter(
            grad_router.astype(jnp.bfloat16), "expert", scatter_dimension=0, tiled=True
        ).astype(jnp.float32),
        lax.psum_scatter(
            grad_shgate.astype(jnp.bfloat16), "expert", scatter_dimension=0, tiled=True
        ).astype(jnp.float32),
        lax.psum_scatter(
            grad_shup.astype(jnp.bfloat16), "expert", scatter_dimension=0, tiled=True
        ).astype(jnp.float32),
        lax.psum_scatter(
            grad_shdown.astype(jnp.bfloat16), "expert", scatter_dimension=0, tiled=True
        ).astype(jnp.float32),
    )
    tok_sum, out_gain_in, out_wlatent, out_gain_lat, out_gain_mid, out_router = (
        lax.psum_scatter(
            tok_part.astype(jnp.bfloat16), "tensor", scatter_dimension=0, tiled=True
        ).astype(jnp.float32),
        lax.psum_scatter(
            part_gain_in.astype(jnp.bfloat16), "tensor", scatter_dimension=0, tiled=True
        ).astype(jnp.float32),
        lax.psum_scatter(
            part_wlatent.astype(jnp.bfloat16), "tensor", scatter_dimension=0, tiled=True
        ).astype(jnp.float32),
        lax.psum_scatter(
            part_gain_lat.astype(jnp.bfloat16), "tensor", scatter_dimension=0, tiled=True
        ).astype(jnp.float32),
        lax.psum_scatter(
            part_gain_mid.astype(jnp.bfloat16), "tensor", scatter_dimension=0, tiled=True
        ).astype(jnp.float32),
        lax.psum_scatter(
            part_router.astype(jnp.bfloat16), "tensor", scatter_dimension=0, tiled=True
        ).astype(jnp.float32),
    )
    rows_part = seq_len // tensor_count
    tokens_grad = (
        tok_sum + lax.dynamic_slice_in_dim(grad_resid, tensor_pos * rows_part, rows_part, 0)
    ).astype(jnp.bfloat16)
    return (
        mixed,
        tokens_grad,
        out_gain_in,
        out_wquery,
        out_wlatent,
        out_gain_lat,
        out_wkeyval,
        out_wout,
        out_gain_mid,
        out_router,
        out_shgate,
        out_shup,
        out_shdown,
        grad_wgate_x,
        grad_wup_x,
        grad_down_x,
    )


def solution(mesh):
    in_specs = (
        P("expert", None),
        P("expert", None),
        P("expert", None),
        P("expert", None),
        P("expert"),
        P("expert", "tensor"),
        P("expert", None),
        P("expert"),
        P("expert", "tensor"),
        P("expert", "tensor"),
        P("expert"),
        P("expert", None),
        P("expert", "tensor"),
        P("expert", "tensor"),
        P("expert", "tensor"),
        P("expert", None, "tensor"),
        P("expert", None, "tensor"),
        P("expert", "tensor", None),
    )
    out_specs = (
        P("expert", "tensor"),
        P(("expert", "tensor"), None),
        P(("expert", "tensor")),
        P("expert", "tensor"),
        P(("expert", "tensor"), None),
        P(("expert", "tensor")),
        P("expert", "tensor"),
        P("expert", "tensor"),
        P(("expert", "tensor")),
        P(("expert", "tensor"), None),
        P("expert", "tensor"),
        P("expert", "tensor"),
        P("expert", "tensor"),
        P("expert", None, "tensor"),
        P("expert", None, "tensor"),
        P("expert", "tensor", None),
    )
    return jax.shard_map(local, mesh=mesh, in_specs=in_specs, out_specs=out_specs, check_vma=False)
```

profile of v0, /device:TPU:0, one launch (start us, length us, event | category | flops | bytes accessed | tf_op | source)
XLA Modules:
  0.0 3413.4 jit_solution(3630674490847471999)
XLA Ops:
  16.9 23.3 all-reduce
  73.0 34.5 %all-gather.12.cloned.1.call-done = bf16[512,1024]{1,0:T(8,128)(2,1)} async-done(((bf16[64,1024]{1,0:T(8,128)(2,1)}), bf16[512,1024]{1,0:T(8,128)(2,1)}) %all-gather.12.cloned.1.call-update) | async-done | bytes 1048592 | tf_op jit(solution)/shard_map/all_gather | solution.py:142
  119.9 48.9 %all-gather.14.cloned.1.call-done = bf16[2048,768]{1,0:T(8,128)(2,1)} async-done(((bf16[256,768]{1,0:T(8,128)(2,1)}), bf16[2048,768]{1,0:T(8,128)(2,1)}) %all-gather.14.cloned.1.call-update) | async-done | bytes 3145744 | tf_op jit(solution)/shard_map/all_gather | solution.py:139
  179.3 39.5 %all-gather.16.cloned.1.call-done = bf16[2048,512]{1,0:T(8,128)(2,1)} async-done(((bf16[256,512]{1,0:T(8,128)(2,1)}), bf16[2048,512]{1,0:T(8,128)(2,1)}) %all-gather.16.cloned.1.call-update) | async-done | bytes 2097168 | tf_op jit(solution)/shard_map/all_gather | solution.py:143
  241.8 21.6 scatter_custom_fusion.1
  281.5 40.7 %gather_fusion = bf16[5120,2048]{1,0:T(8,128)(2,1)} fusion(bf16[512,2048]{1,0:T(8,128)(2,1)} %multiply_convert_fusion.2, s32[5120]{0:T(1024)S(1)} %fusion.99), kind=kCustom, calls=%fused_computation | custom fusion | bytes 41963520 | tf_op jit(solution)/shard_map/gather | solution.py:226
  332.4 456.9 %all_to_all.20 = bf16[8,2,320,2048]{3,2,1,0:T(8,128)(2,1)} all-to-all(bf16[8,2,320,2048]{3,2,1,0:T(8,128)(2,1)S(1)} %broadcast_multiply_fusion), channel_id=1, replica_groups=mesh['expert'=8,'tensor'=4] {'expert'}, dimensions={0} | all-to-all | bytes 41943040 | tf_op jit(solution)/shard_map/all_to_all | solution.py:85
  806.5 20.3 fusion.14
  870.8 41.3 %gather_fusion.2 = f32[5120,2048]{1,0:T(8,128)} fusion(f32[512,2048]{1,0:T(8,128)} %convert_element_type.254, s32[5120]{0:T(1024)S(1)} %fusion.99), kind=kCustom, calls=%fused_computation.2 | custom fusion | bytes 83906560 | tf_op jit(solution)/shard_map/gather | solution.py:259
  912.1 426.2 %all_gather.43 = bf16[2048,16]{0,1:T(8,128)(2,1)S(1)} all-gather(bf16[256,16]{0,1:T(8,128)(2,1)S(1)} %copy-done.81), channel_id=1, replica_groups=mesh['expert'=8,'tensor'=4] {'expert'}, dimensions={0}, use_global_device_ids=true | all-gather | bytes 73728 | tf_op jit(solution)/shard_map/all_gather | solution.py:145
  1341.9 33.5 gather_fusion.1
  1375.4 20.3 reshape.350
  1437.2 452.2 %all_to_all.21 = bf16[8,2,320,2048]{3,2,1,0:T(8,128)(2,1)} all-to-all(bf16[8,2,320,2048]{3,2,1,0:T(8,128)(2,1)S(1)} %multiply_convert_fusion), channel_id=1, replica_groups=mesh['expert'=8,'tensor'=4] {'expert'}, dimensions={0} | all-to-all | bytes 41943040 | tf_op jit(solution)/shard_map/all_to_all | solution.py:85
  1889.4 20.6 fusion.13
  1910.0 19.3 fusion.51
  1929.4 24.2 fusion
  1980.0 383.1 %all-gather.20.cloned.1.call-done = bf16[2048,704]{0,1:T(8,128)(2,1)} async-done(((bf16[256,704]{0,1:T(8,128)(2,1)}), bf16[2048,704]{0,1:T(8,128)(2,1)}) %all-gather.20.cloned.1.call-update) | async-done | bytes 2883600 | tf_op jit(solution)/shard_map/all_gather | solution.py:147
  2367.7 143.8 %all-gather.18.cloned.1.call-done = bf16[2048,704]{0,1:T(8,128)(2,1)} async-done(((bf16[256,704]{0,1:T(8,128)(2,1)}), bf16[2048,704]{0,1:T(8,128)(2,1)}) %all-gather.18.cloned.1.call-update) | async-done | bytes 2883600 | tf_op jit(solution)/shard_map/all_gather | solution.py:146
  2516.1 55.9 %all-gather.22.cloned.1.call-done = bf16[2048,704]{0,1:T(8,128)(2,1)} async-done(((bf16[256,704]{0,1:T(8,128)(2,1)}), bf16[2048,704]{0,1:T(8,128)(2,1)}) %all-gather.22.cloned.1.call-update) | async-done | bytes 2883600 | tf_op jit(solution)/shard_map/all_gather | solution.py:148
  2586.3 33.7 gather_fusion.3
  2620.0 22.2 reshape.354
  2673.4 48.0 %all-reduce.14.cloned.1.call-done = bf16[512,2048]{1,0:T(8,128)(2,1)} async-done(((bf16[512,2048]{1,0:T(8,128)(2,1)}), bf16[512,2048]{1,0:T(8,128)(2,1)}) %all-reduce.14.cloned.1.call-update) | async-done | bytes 2097168 | tf_op jit(solution)/shard_map/psum | solution.py:299
  2808.5 42.3 %reduce-scatter.23.cloned.1.call-done = bf16[256,576]{0,1:T(8,128)(2,1)} async-done(((bf16[2048,576]{0,1:T(8,128)(2,1)}), bf16[256,576]{0,1:T(8,128)(2,1)}) %reduce-scatter.23.cloned.1.call-update) | async-done | bytes 294928 | tf_op jit(solution)/shard_map/reduce_scatter | solution.py:396
  2855.9 70.2 %reduce-scatter.31.cloned.1.call-done = bf16[256,704]{0,1:T(8,128)(2,1)} async-done(((bf16[2048,704]{0,1:T(8,128)(2,1)}), bf16[256,704]{0,1:T(8,128)(2,1)}) %reduce-scatter.31.cloned.1.call-update) | async-done | bytes 360464 | tf_op jit(solution)/shard_map/reduce_scatter | solution.py:414
  2928.0 73.6 %reduce-scatter.33.cloned.1.call-done = bf16[256,704]{0,1:T(8,128)(2,1)} async-done(((bf16[2048,704]{0,1:T(8,128)(2,1)}), bf16[256,704]{0,1:T(8,128)(2,1)}) %reduce-scatter.33.cloned.1.call-update) | async-done | bytes 360464 | tf_op jit(solution)/shard_map/reduce_scatter | solution.py:417
  3003.5 73.0 %reduce-scatter.35.cloned.1.call-done = bf16[256,704]{0,1:T(8,128)(2,1)} async-done(((bf16[2048,704]{0,1:T(8,128)(2,1)}), bf16[256,704]{0,1:T(8,128)(2,1)}) %reduce-scatter.35.cloned.1.call-update) | async-done | bytes 360464 | tf_op jit(solution)/shard_map/reduce_scatter | solution.py:420
  3078.4 19.5 reduce-scatter.39.cloned.1.call-done
  3150.0 21.8 all-reduce.7
  3200.3 69.1 %reduce-scatter.27.cloned.1.call-done = bf16[256,512]{1,0:T(8,128)(2,1)} async-done(((bf16[2048,512]{1,0:T(8,128)(2,1)}), bf16[256,512]{1,0:T(8,128)(2,1)}) %reduce-scatter.27.cloned.1.call-update) | async-done | bytes 262160 | tf_op jit(solution)/shard_map/reduce_scatter | solution.py:405
  3271.2 31.3 reduce-scatter.19.cloned.1.call-done
  3304.8 21.1 reduce-scatter.37.cloned.1.call-done
  3327.7 76.5 %reduce-scatter.21.cloned.1.call-done = bf16[256,768]{1,0:T(8,128)(2,1)} async-done(((bf16[2048,768]{1,0:T(8,128)(2,1)}), bf16[256,768]{1,0:T(8,128)(2,1)}) %reduce-scatter.21.cloned.1.call-update) | async-done | bytes 393232 | tf_op jit(solution)/shard_map/reduce_scatter | solution.py:393
  (373 shorter events, 485.8 us)
Async XLA Ops:
  7.2 819.6 %copy-start = (bf16[2,352,2048]{2,1,0:T(8,128)(2,1)S(1)}, bf16[2,352,2048]{2,1,0:T(8,128)(2,1)}, u32[]{:S(2)}) copy-start(bf16[2,352,2048]{2,1,0:T(8,128)(2,1)} %param.35) | copy-start | bytes 8650756
  7.2 58.7 %copy-start.70 = (s32[1,512]{1,0:T(1,128)S(1)}, s32[1,512]{1,0:T(1,128)}, u32[]{:S(2)}) copy-start(s32[1,512]{1,0:T(1,128)} %param.19) | copy-start | bytes 6148
  7.2 60.3 %all-gather.10.cloned.1.call-start = ((), (), s32[]{:S(2)}) async-start(), calls=%async_computation.16 | async-start | bytes 2654208 | tf_op jit(solution)/shard_map/all_gather | solution.py:140
  7.9 99.5 %all-gather.12.cloned.1.call-start = ((), (), s32[]{:S(2)}) async-start(), calls=%async_computation.17 | async-start | bytes 1179648 | tf_op jit(solution)/shard_map/all_gather | solution.py:142
  8.7 160.2 %all-gather.14.cloned.1.call-start = ((), (), s32[]{:S(2)}) async-start(), calls=%async_computation.18 | async-start | bytes 3538944 | tf_op jit(solution)/shard_map/all_gather | solution.py:139
  9.4 209.4 %all-gather.16.cloned.1.call-start = ((), (), s32[]{:S(2)}) async-start(), calls=%async_computation.19 | async-start | bytes 2359296 | tf_op jit(solution)/shard_map/all_gather | solution.py:143
  10.0 265.4 %all-reduce.12.cloned.1.call-start = ((), (), s32[]{:S(2)}) async-start(), calls=%async_computation.20 | async-start | bytes 4194304 | tf_op jit(solution)/shard_map/psum | solution.py:199
  40.1 67.4 %copy-start.73 = (f32[512]{0:T(512)}, f32[512]{0:T(512)S(1)}, u32[]{:S(2)}) copy-start(f32[512]{0:T(512)S(1)} %convert_element_type.235) | copy-start | bytes 6148
  115.8 57.7 %copy-start.16 = (bf16[512,4,128]{2,1,0:T(4,128)(2,1)}, bf16[512,4,128]{2,1,0:T(4,128)(2,1)S(1)}, u32[]{:S(2)}) copy-start(bf16[512,4,128]{2,1,0:T(4,128)(2,1)S(1)} %get-tuple-element.192) | copy-start | bytes 1572868
  332.4 456.9 %copy-start.22 = (bf16[2,2048,352]{1,2,0:T(8,128)(2,1)S(1)}, bf16[2,2048,352]{1,2,0:T(8,128)(2,1)}, u32[]{:S(2)}) copy-start(bf16[2,2048,352]{1,2,0:T(8,128)(2,1)} %param.33) | copy-start | bytes 8650756
  860.6 481.2 %all-to-all-start.1 = ((bf16[8,2,320,2048]{3,2,1,0:T(8,128)(2,1)}), bf16[8,2,320,2048]{3,2,1,0:T(8,128)(2,1)}, u32[]{:S(2)}, u32[]{:S(2)}) async-start(bf16[8,2,320,2048]{3,2,1,0:T(8,128)(2,1)} %copy.143), calls=%async_computation.1 | async-start | bytes 41943040 | tf_op jit(solution)/shard_map/all_to_all | solution.py:89
  870.8 467.5 %copy-start.63 = (s32[3072,1]{0,1:T(1,128)S(1)}, s32[3072,1]{0,1:T(1,128)}, u32[]{:S(2)}) copy-start(s32[3072,1]{0,1:T(1,128)} %copy-done.62) | copy-start | bytes 36868
  870.8 471.0 %copy-start.51 = (s32[512,6]{0,1:T(8,128)S(1)}, s32[512,6]{0,1:T(8,128)}, u32[]{:S(2)}) copy-start(s32[512,6]{0,1:T(8,128)} %param.20) | copy-start | bytes 36868
  1971.2 391.9 %copy-start.2 = (bf16[512,2048]{1,0:T(8,128)(2,1)S(1)}, bf16[512,2048]{1,0:T(8,128)(2,1)}, u32[]{:S(2)}) copy-start(bf16[512,2048]{1,0:T(8,128)(2,1)} %multiply_convert_fusion.2) | copy-start | bytes 6291460
  1971.2 615.1 %all-to-all-start.3 = ((bf16[8,2,320,2048]{3,2,1,0:T(8,128)(2,1)}), bf16[8,2,320,2048]{3,2,1,0:T(8,128)(2,1)}, u32[]{:S(2)}, u32[]{:S(2)}) async-start(bf16[8,2,320,2048]{3,2,1,0:T(8,128)(2,1)} %copy.146), calls=%async_computation.4 | async-start | bytes 41943040 | tf_op jit(solution)/shard_map/all_to_all | solution.py:89
  1977.4 385.6 %all-gather.20.cloned.1.call-start = ((), (), s32[]{:S(2)}) async-start(), calls=%async_computation.22 | async-start | bytes 3244032 | tf_op jit(solution)/shard_map/all_gather | solution.py:147
  1978.0 533.5 %all-gather.18.cloned.1.call-start = ((), (), s32[]{:S(2)}) async-start(), calls=%async_computation.21 | async-start | bytes 3244032 | tf_op jit(solution)/shard_map/all_gather | solution.py:146
  1978.7 593.2 %all-gather.22.cloned.1.call-start = ((), (), s32[]{:S(2)}) async-start(), calls=%async_computation.23 | async-start | bytes 3244032 | tf_op jit(solution)/shard_map/all_gather | solution.py:148
  1979.5 741.9 %all-reduce.14.cloned.1.call-start = ((), (), s32[]{:S(2)}) async-start(), calls=%async_computation.25 | async-start | bytes 4194304 | tf_op jit(solution)/shard_map/psum | solution.py:299
  2671.7 107.0 %reduce-scatter.29.cloned.1.call-start = ((), (), s32[]{:S(2)}) async-start(), calls=%async_computation.31 | async-start | bytes 73728 | tf_op jit(solution)/shard_map/reduce_scatter | solution.py:411
  2673.3 177.4 %reduce-scatter.23.cloned.1.call-start = ((), (), s32[]{:S(2)}) async-start(), calls=%async_computation.28 | async-start | bytes 2654208 | tf_op jit(solution)/shard_map/reduce_scatter | solution.py:396
  2739.1 187.0 %reduce-scatter.31.cloned.1.call-start = ((), (), s32[]{:S(2)}) async-start(), calls=%async_computation.32 | async-start | bytes 3244032 | tf_op jit(solution)/shard_map/reduce_scatter | solution.py:414
  2743.6 258.0 %reduce-scatter.33.cloned.1.call-start = ((), (), s32[]{:S(2)}) async-start(), calls=%async_computation.33 | async-start | bytes 3244032 | tf_op jit(solution)/shard_map/reduce_scatter | solution.py:417
  2746.9 329.6 %reduce-scatter.35.cloned.1.call-start = ((), (), s32[]{:S(2)}) async-start(), calls=%async_computation.34 | async-start | bytes 3244032 | tf_op jit(solution)/shard_map/reduce_scatter | solution.py:420
  2752.4 345.4 %reduce-scatter.39.cloned.1.call-start = ((), (), s32[]{:S(2)}) async-start(), calls=%async_computation.36 | async-start | bytes 81920
  2780.2 367.5 %reduce-scatter.17.cloned.1.call-start = ((), (), s32[]{:S(2)}) async-start(), calls=%async_computation.24 | async-start | bytes 2621440 | tf_op jit(solution)/shard_map/reduce_scatter | solution.py:240
  2787.8 410.9 %reduce-scatter.25.cloned.1.call-start = ((), (), s32[]{:S(2)}) async-start(), calls=%async_computation.29 | async-start | bytes 1179648 | tf_op jit(solution)/shard_map/reduce_scatter | solution.py:402
  2789.6 479.8 %reduce-scatter.27.cloned.1.call-start = ((), (), s32[]{:S(2)}) async-start(), calls=%async_computation.30 | async-start | bytes 2359296 | tf_op jit(solution)/shard_map/reduce_scatter | solution.py:405
  2794.7 507.8 %reduce-scatter.19.cloned.1.call-start = ((), (), s32[]{:S(2)}) async-start(), calls=%async_computation.26 | async-start | bytes 2621440 | tf_op jit(solution)/shard_map/reduce_scatter | solution.py:425
  2808.4 517.5 %reduce-scatter.37.cloned.1.call-start = ((), (), s32[]{:S(2)}) async-start(), calls=%async_computation.35 | async-start | bytes 409600
  2852.6 551.6 %reduce-scatter.21.cloned.1.call-start = ((), (), s32[]{:S(2)}) async-start(), calls=%async_computation.27 | async-start | bytes 3538944 | tf_op jit(solution)/shard_map/reduce_scatter | solution.py:393
  3179.3 226.9 %copy-start.1 = (bf16[2,352,2048]{2,1,0:T(8,128)(2,1)S(1)}, bf16[2,352,2048]{2,1,0:T(8,128)(2,1)}, u32[]{:S(2)}) copy-start(bf16[2,352,2048]{2,1,0:T(8,128)(2,1)} %param.35) | copy-start | bytes 8650756
  (81 other events, 793.0 us)
Sparse Core Ops, SparseCore 0:
  10.1 56.8 all-gather.9
  69.1 38.3 all-gather.11
  109.7 59.1 all-gather.13
  170.8 47.8 all-gather.15
  223.2 49.8 all-reduce.11
  1980.2 382.8 all-gather.19
  2365.3 146.1 all-gather.17
  2513.7 58.1 all-gather.21
  2671.8 49.5 all-reduce.13
  2724.9 53.7 reduce-scatter.28
  2782.2 68.4 reduce-scatter.22
  2854.7 71.3 reduce-scatter.30
  2930.2 71.3 reduce-scatter.32
  3005.0 71.3 reduce-scatter.34
  3079.3 18.5 reduce-scatter.38
  3100.4 31.4 reduce-scatter.16
  3135.1 63.4 reduce-scatter.24
  3202.5 66.9 reduce-scatter.26
  3272.1 30.4 reduce-scatter.18
  3305.5 20.3 reduce-scatter.36
  3329.9 74.2 reduce-scatter.20
where the time goes:
time: 3430 us; the launch traced here: 3410 us
  blocking collectives  1420 us (41%)
  waiting for transfers between devices  1260 us (37%)
  local copies, waits for them, and re-layouts  300 us (9%)
  matrix products  295 us (9%)
  other arithmetic  99.2 us (3%)
    all_to_all x2, blocking collectives, send_rows(): lax.all_to_all(rows_in, 'expert', split_axis=0, concat_axis=0, tiled=True)  909 us
    all_gather x1, blocking collectives, local(): lax.all_gather(w_router, 'expert', axis=0, tiled=True)  426 us
    all_gather x1, waiting for transfers between devices, local(): lax.all_gather(shared_up, 'expert', axis=0, tiled=True)  383 us
    all_gather x1, waiting for transfers between devices, local(): lax.all_gather(shared_gate, 'expert', axis=0, tiled=True)  144 us
    reduce_scatter x1, waiting for transfers between devices, local(): lax.psum_scatter(grad_wquery.astype(jnp.bfloat16), 'expert', scatter_dime...  76.5 us
    reduce_scatter x1, waiting for transfers between devices, local(): lax.psum_scatter(grad_shup.astype(jnp.bfloat16), 'expert', scatter_dimens...  73.6 us
    reduce_scatter x1, waiting for transfers between devices, local(): lax.psum_scatter(grad_shdown.astype(jnp.bfloat16), 'expert', scatter_dime...  73 us
    reduce_scatter x1, waiting for transfers between devices, local(): lax.psum_scatter(grad_shgate.astype(jnp.bfloat16), 'expert', scatter_dime...  70.2 us
  transfers between devices with their start and end apart: 23, of which 18 were waited for; matrix products, arithmetic and copies ran while one was open for 8% of the time, Pallas kernels for 0%

commit v1 on v0

v1 whole, which is shorter than its diff:
```python
import itertools
import math

import jax
import jax.numpy as jnp
from jax import lax
from jax.experimental import pallas as pl
from jax.experimental.pallas import tpu as pltpu
from jax.sharding import PartitionSpec as P

D = 2048
NOPE = 128
ROPE = 64
VD = 128
KVR = 512
TOP = 6


EPS = 1e-06
ROUTE_SCALE = 2.446
THETA = 50000.0
NEG = -1e30
HIGH = lax.Precision.HIGHEST


def inv_rms(vec_in):
    return lax.rsqrt(jnp.mean(vec_in * vec_in, axis=-1, keepdims=True) + EPS)


def doc_positions(seg_ids):
    row_index = jnp.arange(seg_ids.shape[0], dtype=jnp.int32)
    starts = jnp.concatenate(
        [jnp.ones((1,), jnp.int32), (seg_ids[1:] != seg_ids[:-1]).astype(jnp.int32)]
    )
    first_idx = lax.cummax(jnp.where(starts > 0, row_index, jnp.zeros_like(row_index)), axis=0)
    return row_index - first_idx


def rope_tables(positions):
    half_dim = ROPE // 2
    freqs = THETA ** (-(jnp.arange(half_dim, dtype=jnp.float32) * 2.0 / ROPE))
    angles = positions.astype(jnp.float32)[:, None] * freqs[None, :]
    return (jnp.cos(angles), jnp.sin(angles))


def rotate(vec_in, cos_tab, sin_tab):
    half_dim = vec_in.shape[-1] // 2
    first_h = vec_in[..., :half_dim]
    second_h = vec_in[..., half_dim:]
    return jnp.concatenate(
        [first_h * cos_tab - second_h * sin_tab, first_h * sin_tab + second_h * cos_tab], axis=-1
    )


def unrotate(grad_in, cos_tab, sin_tab):
    half_dim = grad_in.shape[-1] // 2
    first_g = grad_in[..., :half_dim]
    second_g = grad_in[..., half_dim:]
    return jnp.concatenate(
        [first_g * cos_tab + second_g * sin_tab, second_g * cos_tab - first_g * sin_tab], axis=-1
    )


def dot_plain(left_m, right_m):
    return jnp.dot(left_m, right_m, preferred_element_type=jnp.float32)


def dot_last(left_m, right_m):
    return lax.dot_general(
        left_m, right_m, (((1,), (1,)), ((), ())), preferred_element_type=jnp.float32
    )


def dot_first(left_m, right_m):
    return lax.dot_general(
        left_m, right_m, (((0,), (0,)), ((), ())), preferred_element_type=jnp.float32
    )


def norm_back(field_in, inv_scale, gain_f, grad_in):
    scaled = grad_in * gain_f
    grad_field = inv_scale * scaled - field_in * inv_scale**3 * jnp.mean(
        field_in * scaled, axis=-1, keepdims=True
    )
    grad_gain = jnp.sum(grad_in * field_in * inv_scale, axis=0)
    return (grad_field, grad_gain)


MESH = pl.DeviceIdType.MESH
VMEM_BYTES = 56 * 1024 * 1024


def parent_of(key, order):
    for place in range(len(order) - 1, -1, -1):
        if key[place]:
            return key[:place] + (key[place] - 1,) + key[place + 1 :], order[place]
    return None, None


def held(key, order, axes):
    return all(by == 0 or axis in axes for axis, by in zip(order, key))


def hop_order(items, sizes, eager):
    pace = {"z": 22.0, "y": 22.0, "x": 22.0, "c": 5.0}
    hops, below = {}, {}
    for number, (order, size, axes) in enumerate(items):
        for key in itertools.product(*[range(sizes[axis]) for axis in order]):
            if not held(key, order, axes):
                before, axis = parent_of(key, order)
                hops[(number, key)] = ((number, before), axis, size * pace[axis])
    for hop in hops:
        at = hop
        while at in hops:
            below[at] = below.get(at, 0) + hops[hop][2]
            at = hops[at][0]
    free, arrived, started = {}, {}, []
    waiting = sorted(hops)
    while waiting:
        best = None
        for hop in waiting:
            before, axis, cost = hops[hop]
            if before in hops and before not in arrived:
                continue
            start = max(free.get(axis, 0.0), arrived.get(before, 0.0))
            rank = (start, -below[hop], hop)
            if best is None or rank < best[0]:
                best = (rank, hop)
        (start, _, _), hop = best
        waiting.remove(hop)
        before, axis, cost = hops[hop]
        free[axis] = start + cost
        arrived[hop] = start + cost + 1.5
        started.append((arrived.get(before, 0.0) if eager else start, -below[hop], hop))
    started = sorted(started)
    return [(hop, hops[hop][0], hops[hop][1]) for _, _, hop in started], [at for at, _, _ in started]


def place_of(sizes):
    e_pos, t_pos = lax.axis_index("expert"), lax.axis_index("tensor")
    here = {"z": e_pos // sizes["y"], "y": e_pos % sizes["y"], "x": t_pos // sizes["c"], "c": t_pos % sizes["c"]}

    def device(coords):
        return (coords["z"] * sizes["y"] + coords["y"], coords["x"] * sizes["c"] + coords["c"])

    def moved(axis, by):
        there = dict(here)
        there[axis] = lax.rem(here[axis] + (by % sizes[axis]), sizes[axis])
        return there

    return here, device, moved


def owner_of(here, key, order, sizes):
    there = dict(here)
    for axis, by in zip(order, key):
        if by:
            there[axis] = lax.rem(here[axis] + (sizes[axis] - by), sizes[axis])
    return there


def enter(axes, moved, device, sizes):
    barrier = pltpu.get_barrier_semaphore()
    count = 0
    for axis in axes:
        for by in (1, -1) if sizes[axis] > 2 else (1,):
            pl.semaphore_signal(barrier, inc=1, device_id=device(moved(axis, by)), device_id_type=MESH)
            count += 1
    pl.semaphore_wait(barrier, count)


def part_rows(ref, start, rows):
    return ref.at[pl.ds(pl.multiple_of(start, 16), rows)]


def index_of(coords, order, sizes):
    number = 0
    for axis in "zyxc":
        if axis in order:
            number = number * sizes[axis] + coords[axis]
    return number


def held_blocks(items, sizes):
    blocks = []
    for number, (order, _, _, _, axes, _, _) in enumerate(items):
        for key in itertools.product(*[range(sizes[axis]) for axis in order]):
            if held(key, order, axes):
                blocks.append((number, key))
    return blocks


def gather_kernel(items, sizes, hops, *refs):
    n = len(items)
    ins, outs = refs[:n], refs[n : 2 * n]
    own_sem, send_sem, recv_sem = refs[2 * n :]
    here, device, moved = place_of(sizes)

    def slot(number, key):
        order, rows, pitch, base = items[number][:4]
        owner = owner_of(here, key, order, sizes)
        return part_rows(outs[number], index_of(owner, order, sizes) * pitch + base, rows)

    def source(number, key):
        order, rows, _, _, axes, pitch, base = items[number]
        if not held(key, order, axes):
            return slot(number, key)
        owner = owner_of(here, key, order, sizes)
        return part_rows(ins[number], index_of(owner, axes, sizes) * pitch + base, rows)

    place = {hop: at for at, (hop, _, _) in enumerate(hops)}

    def hop_copy(hop, src, axis, dst):
        at = place[hop]
        return pltpu.make_async_remote_copy(
            src_ref=src,
            dst_ref=dst,
            send_sem=send_sem.at[at],
            recv_sem=recv_sem.at[at],
            device_id=device(moved(axis, 1)),
            device_id_type=MESH,
        )

    own = [
        pltpu.make_async_copy(source(*block), slot(*block), own_sem.at[i])
        for i, block in enumerate(held_blocks(items, sizes))
    ]
    for copy in own:
        copy.start()
    enter(sorted({axis for _, _, axis in hops}), moved, device, sizes)
    arrived, sent = set(), []

    def await_block(hop, axis):
        if hop in place and hop not in arrived:
            arrived.add(hop)
            block = slot(*hop)
            hop_copy(hop, block, axis, block).wait_recv()

    axis_of = {hop: axis for hop, _, axis in hops}
    for hop, before, axis in hops:
        if before in place:
            await_block(before, axis_of[before])
        copy = hop_copy(hop, source(*before), axis, slot(*before))
        copy.start()
        sent.append(copy)
    for hop, _, axis in hops:
        await_block(hop, axis)
    for copy in sent:
        copy.wait_send()
    for copy in own:
        copy.wait()


def gather(arrays, plans, sizes, collective_id):
    n = len(plans)
    items = [plan[1:] for plan in plans]
    cost = [(plan[1], plan[2] * arrays[plan[0]].shape[1] * 2e-6, plan[5]) for plan in plans]
    hops, _ = hop_order(cost, sizes, True)
    ids = sorted({plan[0] for plan in plans})
    shapes = []
    for a in ids:
        rows = sum(p[2] * math.prod(sizes[axis] for axis in p[1]) for p in plans if p[0] == a)
        shapes.append(jax.ShapeDtypeStruct((rows, arrays[a].shape[1]), arrays[a].dtype))

    def kernel(*refs):
        ins = {a: refs[i] for i, a in enumerate(ids)}
        outs = {a: refs[len(ids) + i] for i, a in enumerate(ids)}
        rest = refs[2 * len(ids) :]
        gather_kernel(
            items, sizes, hops, *[ins[p[0]] for p in plans], *[outs[p[0]] for p in plans], *rest
        )

    return pl.pallas_call(
        kernel,
        out_shape=shapes,
        in_specs=[pl.BlockSpec(memory_space=pl.ANY)] * len(ids),
        out_specs=[pl.BlockSpec(memory_space=pl.ANY)] * len(ids),
        scratch_shapes=[
            pltpu.SemaphoreType.DMA((len(held_blocks(items, sizes)),)),
            pltpu.SemaphoreType.DMA((len(hops),)),
            pltpu.SemaphoreType.DMA((len(hops),)),
        ],
        compiler_params=pltpu.CompilerParams(
            collective_id=collective_id, has_side_effects=True, vmem_limit_bytes=VMEM_BYTES
        ),
    )(*[arrays[a] for a in ids])


def scatter(arrays, plans, sizes, collective_id):
    n_arrays = len(arrays)
    cost = [(order, rows * arrays[a].shape[1] * 2e-6, "") for a, order, rows, _, _ in plans]
    hops = hop_order(cost, sizes, False)[0][::-1]
    place = {hop: at for at, (hop, _, _) in enumerate(hops)}
    children = {}
    for hop, before, _ in hops:
        children.setdefault(before, []).append(hop)
    counts = {a: math.prod(sizes[axis] for axis in order) for a, order, _, _, _ in plans}
    slots, received = {}, [0] * n_arrays
    for hop, _, _ in hops:
        a, _, rows, _, _ = plans[hop[0]]
        slots[hop] = received[a]
        received[a] += rows
    shapes = [
        jax.ShapeDtypeStruct((v.shape[0] // counts[a], v.shape[1]), jnp.float32)
        for a, v in enumerate(arrays)
    ]

    def kernel(*refs):
        ins, outs = refs[:n_arrays], refs[n_arrays : 2 * n_arrays]
        parts, got = refs[2 * n_arrays : 3 * n_arrays], refs[3 * n_arrays : 4 * n_arrays]
        load_sem, send_sem, recv_sem = refs[4 * n_arrays :]
        here, device, moved = place_of(sizes)
        loads = [pltpu.make_async_copy(ins[a], parts[a], load_sem.at[a]) for a in range(n_arrays)]
        for copy in loads:
            copy.start()
        enter(sorted({axis for _, _, axis in hops}), moved, device, sizes)

        def own_start(number, key):
            _, order, _, pitch, shift = plans[number]
            owner = owner_of(here, key, order, sizes)
            return pl.multiple_of(index_of(owner, order, sizes) * pitch + shift, 16)

        def hop_copy(hop, axis):
            a, _, rows, _, _ = plans[hop[0]]
            return pltpu.make_async_remote_copy(
                src_ref=parts[a].at[pl.ds(own_start(*hop), rows)],
                dst_ref=got[a].at[pl.ds(slots[hop], rows)],
                send_sem=send_sem.at[place[hop]],
                recv_sem=recv_sem.at[place[hop]],
                device_id=device(moved(axis, -1)),
                device_id_type=MESH,
            )

        axis_of = {hop: axis for hop, _, axis in hops}
        loaded = set()

        def summed(number, key):
            a, _, rows, _, _ = plans[number]
            if a not in loaded:
                loaded.add(a)
                loads[a].wait()
            return a, rows, own_start(number, key), children.get((number, key), [])

        sent = []
        for hop, before, axis in hops:
            a, rows, start, below = summed(*hop)
            for child in below:
                hop_copy(child, axis_of[child]).wait_recv()
            if below:
                step = 16
                ref, buf = parts[a], got[a]

                @pl.loop(0, rows // step)
                def _(i, ref=ref, buf=buf, start=start, below=below):
                    at = pl.ds(pl.multiple_of(start + i * step, 16), step)
                    total = ref[at, :].astype(jnp.float32)
                    for child in below:
                        more = pl.ds(pl.multiple_of(slots[child] + i * step, 16), step)
                        total = total + buf[more, :].astype(jnp.float32)
                    ref[at, :] = total.astype(ref.dtype)

            copy = hop_copy(hop, axis)
            copy.start()
            sent.append(copy)
        for number, (a, order, rows, pitch, shift) in enumerate(plans):
            key = (0,) * len(order)
            a, rows, start, below = summed(number, key)
            for child in below:
                hop_copy(child, axis_of[child]).wait_recv()
            step = 16
            ref, buf, out = parts[a], got[a], outs[a]

            @pl.loop(0, rows // step)
            def _(i, ref=ref, buf=buf, out=out, start=start, below=below, shift=shift):
                total = ref[pl.ds(pl.multiple_of(start + i * step, 16), step), :].astype(jnp.float32)
                for child in below:
                    more = pl.ds(pl.multiple_of(slots[child] + i * step, 16), step)
                    total = total + buf[more, :].astype(jnp.float32)
                out[pl.ds(pl.multiple_of(shift + i * step, 16), step), :] = total

        for copy in sent:
            copy.wait_send()

    return pl.pallas_call(
        kernel,
        out_shape=shapes,
        in_specs=[pl.BlockSpec(memory_space=pl.ANY)] * n_arrays,
        out_specs=[pl.BlockSpec(memory_space=pltpu.VMEM)] * n_arrays,
        scratch_shapes=[pltpu.VMEM(v.shape, v.dtype) for v in arrays]
        + [pltpu.VMEM((max(received[a], 16), v.shape[1]), v.dtype) for a, v in enumerate(arrays)]
        + [
            pltpu.SemaphoreType.DMA((n_arrays,)),
            pltpu.SemaphoreType.DMA((len(hops),)),
            pltpu.SemaphoreType.DMA((len(hops),)),
        ],
        compiler_params=pltpu.CompilerParams(
            collective_id=collective_id, has_side_effects=True, vmem_limit_bytes=VMEM_BYTES
        ),
    )(*arrays)


SIZES = {"z": 4, "y": 2, "x": 2, "c": 2}


def direct():
    return lax.axis_size("expert") == 8 and lax.axis_size("tensor") == 4


def halves(a, order_a, order_b, rows):
    return [(a, order_a, rows // 2, rows, 0), (a, order_b, rows // 2, rows, rows // 2)]


def gather_tensor(part, collective_id):
    if not direct():
        return lax.all_gather(part, "tensor", axis=0, tiled=True)
    plans = [plan + ("", 0, plan[4]) for plan in halves(0, "xc", "xc", part.shape[0])]
    return gather([part], plans, SIZES, collective_id)[0]


def scatter_tensor(whole, collective_id):
    if not direct():
        part = lax.psum_scatter(whole, "tensor", scatter_dimension=0, tiled=True)
        return part.astype(jnp.float32)
    return scatter([whole], halves(0, "xc", "xc", whole.shape[0] // 4), SIZES, collective_id)[0]


def slot_events(items, sizes, chunk_of, n_chunks, per_chunk, reverse, tau=1.6):
    speed = {"z": 1.0, "y": 1.0, "x": 1.0, "c": 5.0}
    hops = {}
    for number, (order, cost) in enumerate(items):
        for key in itertools.product(*[range(sizes[axis]) for axis in order]):
            before, axis = parent_of(key, order)
            if before is not None:
                hops[(number, key)] = ((number, before), axis, cost / speed[axis])
    children, depth = {}, {}
    for hop, (before, _, _) in hops.items():
        children.setdefault(before, []).append(hop)
    for hop in hops:
        at = hop
        while at in hops:
            if reverse:
                depth[hop] = depth.get(hop, 0) + hops[at][2]
            else:
                depth[at] = depth.get(at, 0) + hops[hop][2]
            at = hops[at][0]
    free, arrived, now = {}, {}, 8.0
    waiting = sorted(hops, key=lambda hop: (-depth[hop], hop))
    events = [[] for _ in range(n_chunks * per_chunk + 1)]

    def needs(hop):
        if reverse:
            return children.get(hop, [])
        return [hops[hop][0]] if hops[hop][0] in hops else []

    def start_ready(slot, computed):
        for hop in list(waiting):
            if reverse and chunk_of(*hop) >= computed:
                continue
            if all(other in arrived and arrived[other] <= now for other in needs(hop)):
                waiting.remove(hop)
                _, axis, cost = hops[hop]
                begin = max(free.get(axis, 0.0), now)
                free[axis] = begin + cost
                arrived[hop] = begin + cost + 2.0
                events[slot].append(hop)

    for chunk in range(n_chunks):
        for part in range(per_chunk):
            slot = chunk * per_chunk + part
            start_ready(slot, chunk)
            if part == 0 and not reverse:
                blocks = [hop for hop in hops if chunk_of(*hop) == chunk]
                while not all(hop in arrived and arrived[hop] <= now for hop in blocks):
                    now = min(t for t in arrived.values() if t > now)
                    start_ready(slot, chunk)
            now += tau
    while waiting:
        start_ready(n_chunks * per_chunk, n_chunks)
        if waiting:
            now = min(t for t in arrived.values() if t > now)
    axis_of = {hop: hops[hop][1] for hop in hops}
    before_of = {hop: hops[hop][0] for hop in hops}
    return events, axis_of, before_of, children


ORDERS = ("zyxc", "zxyc")
CHUNK = 256
PER = 3


def chunk_number(reverse):
    def of(number, key):
        coord = dict(zip(ORDERS[number], key))
        if reverse:
            return (3 - coord["z"]) * 4 + (1 - coord["y"]) * 2 + number
        return coord["z"] * 4 + coord["y"] * 2 + number

    return of


def chunk_start(step, here, half_rows, reverse):
    dz, dy, half = step // 4, (step // 2) % 2, step % 2
    if reverse:
        dz, dy = 3 - dz, 1 - dy
    z, y = lax.rem(here["z"] + 4 - dz, 4), lax.rem(here["y"] + 2 - dy, 2)
    return pl.multiple_of(half * half_rows + (z * 2 + y) * CHUNK, CHUNK)


def run_events(events, step, part, act):
    for chunk in range((len(events) - 1) // PER):
        todo = events[chunk * PER + part]
        if todo:

            @pl.when(step == chunk)
            def _(todo=todo):
                act(todo)


def weight_copies(gate, up, down, shared, w_gate_up, w_down, segments, sem):
    n_routed, units, _ = gate.shape
    n_from, _, shared_units, cols = shared.shape
    total = sum(segments)
    copies = []
    for which, (src, dst, base) in enumerate(
        [(gate, w_gate_up, 0), (up, w_gate_up, total), (down, w_down, 0)]
    ):
        for i in range(n_routed):
            start = base + sum(segments[:i])
            copies.append((src.at[i], dst.at[pl.ds(start, units)]))
            dst[start + units : start + segments[i], :] = jnp.zeros(
                (segments[i] - units, dst.shape[1]), dst.dtype
            )
        start = base + sum(segments[:-1])
        for i in range(n_from):
            copies.append(
                (shared.at[i, which], dst.at[pl.ds(start, shared_units), pl.ds(i * cols, cols)])
            )
        dst[start + shared_units : start + segments[-1], :] = jnp.zeros(
            (segments[-1] - shared_units, dst.shape[1]), dst.dtype
        )
    return [pltpu.make_async_copy(src, dst, sem.at[i]) for i, (src, dst) in enumerate(copies)]


def n_weight_copies(gate, shared):
    return 3 * (gate.shape[0] + shared.shape[0])


def dot_nt(left, right):
    return lax.dot_general(left, right, (((1,), (1,)), ((), ())), preferred_element_type=jnp.float32)


def mixture_forward(normed_mid, dy_all, mask_all, weights_w, router_w, here_units, collective_id):
    sizes = SIZES
    part_rows_n, width = normed_mid.shape
    block = part_rows_n // 2
    n_rows = part_rows_n * 32
    half_rows = n_rows // 2
    units = sum(here_units)
    n_chunks = n_rows // CHUNK
    seg = here_units
    n_copies = n_weight_copies(weights_w[0], weights_w[3])
    n_routed = len(seg) - 1
    events, axis_of, before_of, _ = slot_events(
        [(order, 8.0) for order in ORDERS], sizes, chunk_number(False), n_chunks, PER, False
    )
    place = {hop: at for at, hop in enumerate(sorted(axis_of))}
    bf = jnp.bfloat16
    arrived, actions = set(), []
    for number, todo in enumerate(events):
        actions.append([])
        needed = [(before_of[hop], hop) for hop in todo]
        if number % PER == 0 and number < n_chunks * PER:
            mine = [hop for hop in axis_of if chunk_number(False)(*hop) == number // PER]
            needed += [(hop, None) for hop in sorted(mine)]
        for block_key, hop in needed:
            if block_key in axis_of and block_key not in arrived:
                arrived.add(block_key)
                actions[-1].append((block_key, True))
            if hop is not None:
                actions[-1].append((hop, False))

    def kernel(
        nm, dy, mask, gate_h, up_h, down_h, shared_h, router_h,
        x_out, hid_out, dgu_out, gg,
        x_vm, wgu, wd, wr, dy_buf, hid_st, dgu_st,
        w_sem, own_sem, dy_sem, x_sem, st_sem, send_sem, recv_sem,
    ):
        here, device, moved = place_of(sizes)
        e_pos = lax.axis_index("expert")

        def slot(number, key):
            owner = owner_of(here, key, ORDERS[number], sizes)
            start = number * half_rows + index_of(owner, "zyxc", sizes) * block
            return x_vm.at[pl.ds(pl.multiple_of(start, block), block)]

        def source(number, key):
            if any(key):
                return slot(number, key)
            return nm.at[pl.ds(number * block, block)]

        def hop_copy(hop, src, dst):
            return pltpu.make_async_remote_copy(
                src_ref=src,
                dst_ref=dst,
                send_sem=send_sem.at[place[hop]],
                recv_sem=recv_sem.at[place[hop]],
                device_id=device(moved(axis_of[hop], 1)),
                device_id_type=MESH,
            )

        weights = weight_copies(gate_h, up_h, down_h, shared_h, wgu, wd, seg, w_sem)
        weights.append(pltpu.make_async_copy(router_h, wr, w_sem.at[n_copies]))
        own = [
            pltpu.make_async_copy(source(i, (0,) * 4), slot(i, (0,) * 4), own_sem.at[i]) for i in range(2)
        ]

        def dy_copy(step):
            at = chunk_start(step, here, half_rows, False)
            return pltpu.make_async_copy(
                dy.at[pl.ds(at, CHUNK)], dy_buf.at[lax.rem(step, 2)], dy_sem.at[lax.rem(step, 2)]
            )

        def x_copy(step):
            at = chunk_start(step, here, half_rows, False)
            return pltpu.make_async_copy(x_vm.at[pl.ds(at, CHUNK)], x_out.at[pl.ds(at, CHUNK)], x_sem.at[step])

        def st_copies(step):
            at = chunk_start(step, here, half_rows, False)
            turn = lax.rem(step, 2)
            return [
                pltpu.make_async_copy(st.at[turn], out.at[pl.ds(at, CHUNK)], st_sem.at[i, turn])
                for i, (st, out) in enumerate([(hid_st, hid_out), (dgu_st, dgu_out)])
            ]

        for copy in own + weights:
            copy.start()
        dy_copy(0).start()
        enter("zyxc", moved, device, sizes)

        def act(todo):
            for hop, wait in todo:
                if wait:
                    hop_copy(hop, slot(*hop), slot(*hop)).wait_recv()
                else:
                    hop_copy(hop, source(*before_of[hop]), slot(*before_of[hop])).start()

        @pl.loop(0, n_chunks)
        def _(step):
            for chunk in range(n_chunks):

                @pl.when(step == chunk)
                def _(chunk=chunk):
                    act(actions[chunk * PER])
                    if chunk == 0:
                        for copy in own + weights:
                            copy.wait()

            turn = lax.rem(step, 2)
            at = chunk_start(step, here, half_rows, False)
            rows = pl.ds(at, CHUNK)
            x_copy(step).start()
            dy_copy(step).wait()

            @pl.when(step + 1 < n_chunks)
            def _():
                dy_copy(step + 1).start()

            logits = jnp.dot(x_vm[rows, :], wr[...], preferred_element_type=jnp.float32)
            chosen = jax.nn.sigmoid(logits) * mask[rows, :].astype(jnp.float32)
            gate_weights = ROUTE_SCALE * chosen / jnp.sum(chosen, axis=1, keepdims=True)
            lane = lax.broadcasted_iota(jnp.int32, (CHUNK, 128), 1)
            scales = []
            for which in range(n_routed):
                mine = jnp.where(lane == e_pos * n_routed + which, gate_weights, 0.0)
                scales.append(jnp.sum(mine, axis=1, keepdims=True))

            @pl.when(step >= 2)
            def _():
                for copy in st_copies(step - 2):
                    copy.wait()

            sums = [jnp.zeros((CHUNK, 128), jnp.float32) for _ in range(n_routed)]
            ends = [sum(seg[: i + 1]) for i in range(len(seg))]
            for number, begin in enumerate(range(0, units, 256)):
                end = min(begin + 256, units)
                g_tile = dot_nt(x_vm[rows, :], wgu[begin:end, :])
                u_tile = dot_nt(x_vm[rows, :], wgu[units + begin : units + end, :])
                h_tile = dot_nt(dy_buf[turn], wd[begin:end, :])
                for at_lane in range(begin, end, 128):
                    which = sum(at_lane >= stop for stop in ends)
                    part = slice(at_lane - begin, at_lane - begin + 128)
                    cols = slice(at_lane, at_lane + 128)
                    more = slice(units + at_lane, units + at_lane + 128)
                    g, u, h = g_tile[:, part], u_tile[:, part], h_tile[:, part]
                    sig = jax.nn.sigmoid(g)
                    silu = g * sig
                    hid = silu * u
                    if which < n_routed:
                        sums[which] = sums[which] + h * hid
                        hid = hid * scales[which]
                        h = h * scales[which]
                    hid_st[turn, :, cols] = hid.astype(bf)
                    dgu_st[turn, :, cols] = (h * u * (sig + silu * (1.0 - sig))).astype(bf)
                    dgu_st[turn, :, more] = (h * silu).astype(bf)
                if number == 1:
                    run_events(actions, step, 1, act)
                    run_events(actions, step, 2, act)

            total = jnp.zeros((CHUNK, 128), jnp.float32)
            for which in range(n_routed):
                mine = jnp.sum(sums[which], axis=1, keepdims=True)
                total = jnp.where(lane == e_pos * n_routed + which, mine, total)
            gg[rows, :] = total.astype(bf)

            for copy in st_copies(step):
                copy.start()

        for step in range(n_chunks):
            x_copy(step).wait()
        for step in (n_chunks - 2, n_chunks - 1):
            for copy in st_copies(step):
                copy.wait()
        for hop in sorted(axis_of):
            hop_copy(hop, source(*before_of[hop]), slot(*before_of[hop])).wait_send()

    any_spec, vm_spec = pl.BlockSpec(memory_space=pl.ANY), pl.BlockSpec(memory_space=pltpu.VMEM)
    return pl.pallas_call(
        kernel,
        out_shape=[
            jax.ShapeDtypeStruct((n_rows, width), bf),
            jax.ShapeDtypeStruct((n_rows, units), bf),
            jax.ShapeDtypeStruct((n_rows, 2 * units), bf),
            jax.ShapeDtypeStruct((n_rows, 128), bf),
        ],
        in_specs=[any_spec, any_spec, vm_spec] + [any_spec] * 5,
        out_specs=[any_spec] * 3 + [vm_spec],
        scratch_shapes=[
            pltpu.VMEM((n_rows, width), bf),
            pltpu.VMEM((2 * units, width), bf),
            pltpu.VMEM((units, width), bf),
            pltpu.VMEM((width, 128), bf),
            pltpu.VMEM((2, CHUNK, width), bf),
            pltpu.VMEM((2, CHUNK, units), bf),
            pltpu.VMEM((2, CHUNK, 2 * units), bf),
            pltpu.SemaphoreType.DMA((n_copies + 1,)),
            pltpu.SemaphoreType.DMA((2,)),
            pltpu.SemaphoreType.DMA((2,)),
            pltpu.SemaphoreType.DMA((n_chunks,)),
            pltpu.SemaphoreType.DMA((2, 2)),
            pltpu.SemaphoreType.DMA((len(axis_of),)),
            pltpu.SemaphoreType.DMA((len(axis_of),)),
        ],
        compiler_params=pltpu.CompilerParams(
            collective_id=collective_id, has_side_effects=True, vmem_limit_bytes=VMEM_BYTES
        ),
    )(normed_mid, dy_all, mask_all, *weights_w, router_w)


def mixture_backward(hidden, grad_gate_up, gate_sums, residual, weights_w, here_units, collective_id):
    sizes = SIZES
    n_rows, units = hidden.shape
    width = weights_w[0].shape[2]
    n_copies = n_weight_copies(weights_w[0], weights_w[3])
    all_width = width + 128
    half_rows = n_rows // 2
    block = n_rows // 64
    n_chunks = n_rows // CHUNK
    events, axis_of, before_of, children = slot_events(
        [(order, 6.9) for order in ORDERS], sizes, chunk_number(True), n_chunks, PER, True
    )
    place = {hop: at for at, hop in enumerate(sorted(axis_of))}
    bf = jnp.bfloat16
    tile_n = width // 4

    def kernel(
        hid_in, dgu_in, gg_in, resid, gate_h, up_h, down_h, shared_h,
        sums, x_out, unit_out,
        parts, got, wgu, wd, hid_b, dgu_b, gg_b, x_st, unit_st,
        w_sem, in_sem, x_sem, unit_sem, send_sem, recv_sem,
    ):
        here, device, moved = place_of(sizes)

        def own_start(number, key):
            owner = owner_of(here, key, ORDERS[number], sizes)
            return pl.multiple_of(number * half_rows + index_of(owner, "zyxc", sizes) * block, block)

        def hop_copy(hop):
            return pltpu.make_async_remote_copy(
                src_ref=parts.at[pl.ds(own_start(*hop), block)],
                dst_ref=got.at[pl.ds(place[hop] * block, block)],
                send_sem=send_sem.at[place[hop]],
                recv_sem=recv_sem.at[place[hop]],
                device_id=device(moved(axis_of[hop], -1)),
                device_id_type=MESH,
            )

        def total_of(number, key, write):
            below = children.get((number, key), [])
            for child in below:
                hop_copy(child).wait_recv()
            start = own_start(number, key)
            tile = 16

            @pl.loop(0, block // tile)
            def _(i):
                at = pl.ds(pl.multiple_of(start + i * tile, tile), tile)
                total = parts[at, :].astype(jnp.float32)
                for child in below:
                    more = pl.ds(pl.multiple_of(place[child] * block + i * tile, tile), tile)
                    total = total + got[more, :].astype(jnp.float32)
                write(i * tile, at, total)

        def keep(offset, at, total):
            parts[at, :] = total.astype(bf)

        def act(todo):
            for hop in todo:
                if children.get(hop):
                    total_of(*hop, keep)
                hop_copy(hop).start()

        weights = weight_copies(gate_h, up_h, down_h, shared_h, wgu, wd, here_units, w_sem)

        def in_copies(step):
            at = pl.ds(chunk_start(step, here, half_rows, True), CHUNK)
            turn = lax.rem(step, 2)
            return [
                pltpu.make_async_copy(src.at[at], dst.at[turn], in_sem.at[i, turn])
                for i, (src, dst) in enumerate([(dgu_in, dgu_b), (hid_in, hid_b), (gg_in, gg_b)])
            ]

        def x_copy(step):
            turn, half = lax.rem(step, 2), step % 2
            at = (chunk_start(step, here, half_rows, True) - half * half_rows) // CHUNK
            return pltpu.make_async_copy(x_st.at[turn], x_out.at[at, :, :, half], x_sem.at[turn])

        def unit_copy(step):
            at = pl.ds(chunk_start(step, here, half_rows, True), CHUNK)
            turn = lax.rem(step, 2)
            return pltpu.make_async_copy(unit_st.at[turn], unit_out.at[:, at], unit_sem.at[turn])

        for copy in in_copies(0) + weights:
            copy.start()
        enter("zyxc", moved, device, sizes)
        for copy in weights:
            copy.wait()

        @pl.loop(0, n_chunks)
        def _(step):
            turn = lax.rem(step, 2)
            at = chunk_start(step, here, half_rows, True)
            rows = pl.ds(at, CHUNK)
            run_events(events, step, 0, act)
            for copy in in_copies(step):
                copy.wait()

            @pl.when(step + 1 < n_chunks)
            def _():
                for copy in in_copies(step + 1):
                    copy.start()

            @pl.when(step >= 2)
            def _():
                unit_copy(step - 2).wait()

            for part in range(2):
                for n in range(part * units, (part + 1) * units, 128):
                    unit_st[turn, n : n + 128, :] = dgu_b[turn, :, n : n + 128].T
                for n in range(part * (width // 2), (part + 1) * (width // 2), tile_n):
                    cols = slice(n, n + tile_n)
                    total = jnp.dot(dgu_b[turn], wgu[:, cols], preferred_element_type=jnp.float32)
                    parts[rows, cols] = total.astype(bf)
                if part == 0:
                    run_events(events, step, 1, act)
            parts[rows, width:] = gg_b[turn]
            run_events(events, step, 2, act)

            @pl.when(step >= 2)
            def _():
                x_copy(step - 2).wait()

            for n in range(0, units, 128):
                unit_st[turn, 2 * units + n : 2 * units + n + 128, :] = hid_b[turn, :, n : n + 128].T
            for n in range(0, width, tile_n):
                cols = slice(n, n + tile_n)
                total = jnp.dot(hid_b[turn], wd[:, cols], preferred_element_type=jnp.float32)
                x_st[turn, n // tile_n] = total.astype(bf).reshape(CHUNK // block, block, tile_n)

            @pl.when(step >= n_chunks - 2)
            def _():
                own = lax.axis_index("tensor")
                for n in range(0, width, tile_n):
                    more = resid[pl.ds(pl.multiple_of(lax.rem(step, 2) * block, block), block), n : n + tile_n]
                    total = x_st[turn, n // tile_n, own].astype(jnp.float32) + more
                    x_st[turn, n // tile_n, own] = total.astype(bf)

            x_copy(step).start()
            unit_copy(step).start()

        act(events[-1])
        for number in range(2):

            def give(offset, at, total, number=number):
                sums[pl.ds(pl.multiple_of(number * block + offset, 16), 16), :] = total

            total_of(number, (0,) * 4, give)
        for step in (n_chunks - 2, n_chunks - 1):
            x_copy(step).wait()
            unit_copy(step).wait()
        for hop in sorted(axis_of):
            hop_copy(hop).wait_send()

    any_spec, vm_spec = pl.BlockSpec(memory_space=pl.ANY), pl.BlockSpec(memory_space=pltpu.VMEM)
    n_hops = len(axis_of)
    return pl.pallas_call(
        kernel,
        out_shape=[
            jax.ShapeDtypeStruct((2 * block, all_width), jnp.float32),
            jax.ShapeDtypeStruct(
                (half_rows // CHUNK, width // tile_n, CHUNK // block, 2, block, tile_n), bf
            ),
            jax.ShapeDtypeStruct((3 * units, n_rows), bf),
        ],
        in_specs=[any_spec] * 3 + [vm_spec] + [any_spec] * 4,
        out_specs=[vm_spec, any_spec, any_spec],
        scratch_shapes=[
            pltpu.VMEM((n_rows, all_width), bf),
            pltpu.VMEM((n_hops * block, all_width), bf),
            pltpu.VMEM((2 * units, width), bf),
            pltpu.VMEM((units, width), bf),
            pltpu.VMEM((2, CHUNK, units), bf),
            pltpu.VMEM((2, CHUNK, 2 * units), bf),
            pltpu.VMEM((2, CHUNK, 128), bf),
            pltpu.VMEM((2, width // tile_n, CHUNK // block, block, tile_n), bf),
            pltpu.VMEM((2, 3 * units, CHUNK), bf),
            pltpu.SemaphoreType.DMA((n_copies,)),
            pltpu.SemaphoreType.DMA((3, 2)),
            pltpu.SemaphoreType.DMA((2,)),
            pltpu.SemaphoreType.DMA((2,)),
            pltpu.SemaphoreType.DMA((n_hops,)),
            pltpu.SemaphoreType.DMA((n_hops,)),
        ],
        compiler_params=pltpu.CompilerParams(
            collective_id=collective_id, has_side_effects=True, vmem_limit_bytes=VMEM_BYTES
        ),
    )(hidden, grad_gate_up, gate_sums, residual, *weights_w)


def final_sums(parts_in, plans, unit_rows, x_all, dy_all, here_units, n_routed, units, shared_units, collective_id):
    sizes = SIZES
    n_arrays = len(parts_in)
    n_rows, width = x_all.shape
    total_units = sum(here_units)
    slab = 256
    n_slabs = width // slab
    sh_pad = -(-shared_units // 16) * 16
    n_steps = 2 * n_slabs
    bf = jnp.bfloat16
    events, axis_of, before_of, children = slot_events(
        [(order, rows * parts_in[a].shape[1] * 44e-6) for a, order, rows, _, _ in plans],
        sizes,
        lambda number, key: -1,
        n_steps,
        1,
        True,
        8.0,
    )
    place = {hop: at for at, hop in enumerate(sorted(axis_of))}
    counts = {a: math.prod(sizes[axis] for axis in order) for a, order, _, _, _ in plans}
    slots, received = {}, [0] * n_arrays
    for hop in sorted(axis_of):
        a, _, rows, _, _ = plans[hop[0]]
        slots[hop] = received[a]
        received[a] += rows

    def kernel(*refs):
        refs = list(refs)

        def take(n):
            got = refs[:n]
            del refs[:n]
            return got

        ins, (unit_h, x_h, dy_h) = take(n_arrays), take(3)
        outs, (g_out, u_out, d_out), sh_outs = take(n_arrays), take(3), take(3)
        parts, got = take(n_arrays), take(n_arrays)
        slab_buf, unit_t, st, sh_st, sh_got = take(5)
        load_sem, unit_sem, slab_sem, st_sem, send_sem, recv_sem, sh_send, sh_recv = refs
        e_pos, t_pos = lax.axis_index("expert"), lax.axis_index("tensor")
        here, device, moved = place_of(sizes)
        loads = [pltpu.make_async_copy(ins[a], parts[a], load_sem.at[a]) for a in range(n_arrays)]

        def own_start(number, key):
            _, order, _, pitch, base = plans[number]
            owner = owner_of(here, key, order, sizes)
            return pl.multiple_of(index_of(owner, order, sizes) * pitch + base, 16)

        def hop_copy(hop):
            a, _, rows, _, _ = plans[hop[0]]
            return pltpu.make_async_remote_copy(
                src_ref=parts[a].at[pl.ds(own_start(*hop), rows)],
                dst_ref=got[a].at[pl.ds(slots[hop], rows)],
                send_sem=send_sem.at[place[hop]],
                recv_sem=recv_sem.at[place[hop]],
                device_id=device(moved(axis_of[hop], -1)),
                device_id_type=MESH,
            )

        def total_of(number, key, write):
            a, _, rows, _, _ = plans[number]
            below = children.get((number, key), [])
            for child in below:
                hop_copy(child).wait_recv()
            start = own_start(number, key)

            @pl.loop(0, rows // 16)
            def _(i):
                at = pl.ds(pl.multiple_of(start + i * 16, 16), 16)
                total = parts[a][at, :].astype(jnp.float32)
                for child in below:
                    more = pl.ds(pl.multiple_of(slots[child] + i * 16, 16), 16)
                    total = total + got[a][more, :].astype(jnp.float32)
                write(a, i * 16, at, total)

        def keep(a, offset, at, total):
            parts[a][at, :] = total.astype(bf)

        def act(todo):
            for hop in todo:
                if children.get(hop):
                    total_of(*hop, keep)
                hop_copy(hop).start()

        def run(step, first, count):
            for number in range(first, first + count):
                if events[number] and number:

                    @pl.when(step == number - first)
                    def _(number=number):
                        act(events[number])

        def slab_copy(src, number, turn, cols=slab):
            start = number * slab
            if not isinstance(number, int):
                start = pl.multiple_of(start, slab)
            return pltpu.make_async_copy(
                src.at[:, pl.ds(start, cols)], slab_buf.at[turn, :, pl.ds(0, cols)], slab_sem.at[turn]
            )

        shared_rows = sum(here_units[:-1])

        def sh_copy(which, to, src):
            return pltpu.make_async_remote_copy(
                src_ref=sh_st.at[which, to],
                dst_ref=sh_got.at[which, src],
                send_sem=sh_send.at[which, to],
                recv_sem=sh_recv.at[which, src],
                device_id=(to, t_pos),
                device_id_type=MESH,
            )

        def give_shared(which, step, part):
            @pl.when(step == e_pos)
            def _():
                sh_got[which, step] = part

            @pl.when(step != e_pos)
            def _():
                sh_st[which, step] = part
                sh_copy(which, step, e_pos).start()

        unit_load = pltpu.make_async_copy(unit_h, unit_t, unit_sem)
        for copy in loads:
            copy.start()
        barrier = pltpu.get_barrier_semaphore()
        n_expert = sizes["z"] * sizes["y"]
        others = [(lax.rem(e_pos + i, n_expert), t_pos) for i in range(1, n_expert)]
        others += [device(moved(axis, 1)) for axis in "xc"]
        for other in others:
            pl.semaphore_signal(barrier, inc=1, device_id=other, device_id_type=MESH)
        pl.semaphore_wait(barrier, len(others))
        for copy in loads:
            copy.wait()
        act(events[0])
        unit_load.start()
        slab_copy(x_h, 0, 0).start()
        unit_load.wait()

        def st_copies(turn, which, number):
            cols = pl.ds(pl.multiple_of(number * slab, slab), slab)
            out = (g_out, u_out, d_out)[which]
            pairs = [
                (st.at[turn, pl.ds(sum(here_units[:i]), units)], out.at[i, :, cols])
                for i in range(n_routed)
            ]
            return [pltpu.make_async_copy(src, dst, st_sem.at[turn, i]) for i, (src, dst) in enumerate(pairs)]

        @pl.loop(0, n_slabs)
        def _(step):
            run(step, 0, n_slabs)
            turn = lax.rem(step, 2)
            slab_copy(x_h, step, turn).wait()

            @pl.when(step + 1 < n_slabs)
            def _():
                slab_copy(x_h, step + 1, 1 - turn).start()

            @pl.when(step + 1 == n_slabs)
            def _():
                slab_copy(dy_h, 0, 1 - turn).start()

            for which in range(2):

                @pl.when(step >= 1)
                def _(which=which):
                    for copy in st_copies(which, which, step - 1):
                        copy.wait()

                st[which] = jnp.dot(
                    unit_t[which * total_units : (which + 1) * total_units, :],
                    slab_buf[turn],
                    preferred_element_type=jnp.float32,
                )
                for copy in st_copies(which, which, step):
                    copy.start()
                give_shared(which, step, st[which, shared_rows : shared_rows + sh_pad, :].astype(bf))

        for which in range(2):
            for copy in st_copies(which, which, n_slabs - 1):
                copy.wait()

        @pl.loop(0, n_slabs)
        def _(step):
            run(step, n_slabs, n_slabs)
            turn = lax.rem(step + n_slabs, 2)
            slab_copy(dy_h, step, turn).wait()

            @pl.when(step + 1 < n_slabs)
            def _():
                slab_copy(dy_h, step + 1, 1 - turn).start()

            half = lax.rem(step, 2)

            @pl.when(step >= 2)
            def _():
                for copy in st_copies(half, 2, step - 2):
                    copy.wait()

            st[half] = jnp.dot(
                unit_t[2 * total_units :, :], slab_buf[turn], preferred_element_type=jnp.float32
            )
            for copy in st_copies(half, 2, step):
                copy.start()
            give_shared(2, step, st[half, shared_rows : shared_rows + sh_pad, :].astype(bf))

        act(events[-1])
        for number, (_, order_n, _, _, base_n) in enumerate(plans):

            def give(a, offset, at, total, base_n=base_n):
                outs[a][pl.ds(pl.multiple_of(base_n + offset, 16), 16), :] = total

            total_of(number, (0,) * len(order_n), give)
        for which in range(3):
            for i in range(1, n_expert):
                other = lax.rem(e_pos + i, n_expert)
                sh_copy(which, other, other).wait_recv()
            for i in range(n_expert):
                sh_outs[which][i * shared_units : (i + 1) * shared_units, :] = sh_got[
                    which, i, :shared_units, :
                ].astype(jnp.float32)
            for i in range(1, n_expert):
                other = lax.rem(e_pos + i, n_expert)
                sh_copy(which, other, other).wait_send()
        for step in (n_slabs - 2, n_slabs - 1):
            for copy in st_copies(step % 2, 2, step):
                copy.wait()
        for hop in sorted(axis_of):
            hop_copy(hop).wait_send()

    f32 = jnp.float32
    shapes = [
        jax.ShapeDtypeStruct((v.shape[0] // counts[a], v.shape[1]), f32) for a, v in enumerate(parts_in)
    ]
    shapes += [jax.ShapeDtypeStruct((n_routed, units, width), f32)] * 3
    shapes += [jax.ShapeDtypeStruct((8 * shared_units, slab), f32)] * 3
    any_spec, vm_spec = pl.BlockSpec(memory_space=pl.ANY), pl.BlockSpec(memory_space=pltpu.VMEM)
    n_hops = len(axis_of)
    return pl.pallas_call(
        kernel,
        out_shape=shapes,
        in_specs=[any_spec] * (n_arrays + 3),
        out_specs=[vm_spec] * n_arrays + [any_spec] * 3 + [vm_spec] * 3,
        scratch_shapes=[pltpu.VMEM(v.shape, v.dtype) for v in parts_in]
        + [pltpu.VMEM((received[a], v.shape[1]), v.dtype) for a, v in enumerate(parts_in)]
        + [
            pltpu.VMEM((2, n_rows, slab), bf),
            pltpu.VMEM((3 * total_units, n_rows), bf),
            pltpu.VMEM((2, total_units, slab), f32),
            pltpu.VMEM((3, 8, sh_pad, slab), bf),
            pltpu.VMEM((3, 8, sh_pad, slab), bf),
            pltpu.SemaphoreType.DMA((n_arrays,)),
            pltpu.SemaphoreType.DMA,
            pltpu.SemaphoreType.DMA((2,)),
            pltpu.SemaphoreType.DMA((2, n_routed)),
            pltpu.SemaphoreType.DMA((n_hops,)),
            pltpu.SemaphoreType.DMA((n_hops,)),
            pltpu.SemaphoreType.DMA((3, 8)),
            pltpu.SemaphoreType.DMA((3, 8)),
        ],
        compiler_params=pltpu.CompilerParams(
            collective_id=collective_id, has_side_effects=True, vmem_limit_bytes=VMEM_BYTES
        ),
    )(*parts_in, unit_rows, x_all, dy_all)


def masked_scores(qn_blk, qr_blk, key_nope, key_rope, seg_blk, seg_ids, first_row):
    block_len = qn_blk.shape[0]
    scores = jnp.einsum("qhd,khd->hqk", qn_blk, key_nope, preferred_element_type=jnp.float32)
    scores = scores + jnp.einsum(
        "qhd,kd->hqk", qr_blk, key_rope, preferred_element_type=jnp.float32
    )
    scores = scores * (NOPE + ROPE) ** (-0.5)
    row_pos = first_row + jnp.arange(block_len, dtype=jnp.int32)
    col_pos = jnp.arange(key_nope.shape[0], dtype=jnp.int32)
    allowed = (seg_blk[:, None] == seg_ids[None, :]) & (row_pos[:, None] >= col_pos[None, :])
    return jnp.where(allowed[None], scores, NEG)


def local(
    tokens,
    segments,
    routes,
    cotangent,
    norm_in,
    w_query,
    w_latent,
    norm_latent,
    w_keyval,
    w_out,
    norm_mid,
    w_router,
    shared_gate,
    shared_up,
    shared_down,
    expert_gate,
    expert_up,
    expert_down,
):
    seq_len = tokens.shape[0]
    n_expert = lax.axis_size("expert")
    n_tensor = lax.axis_size("tensor")
    expert_pos = lax.axis_index("expert")
    tensor_pos = lax.axis_index("tensor")
    experts_all = w_router.shape[1]
    experts_here = expert_gate.shape[0]
    rows_part = seq_len // n_tensor
    both = ("expert", "tensor")

    def my_rows(whole):
        return lax.dynamic_slice_in_dim(whole, tensor_pos * rows_part, rows_part, 0)

    expert_ids = jnp.arange(experts_all, dtype=jnp.int32)
    routed = jnp.any(routes[:, :, None] == expert_ids[None, None, :], axis=1).astype(jnp.bfloat16)
    my_routed = my_rows(routed)

    n_gain, n_lat = norm_in.shape[0], norm_latent.shape[0]
    small = jnp.concatenate([norm_in, norm_mid, norm_latent, w_router.reshape(-1)])
    if direct():
        rows = -(-small.shape[0] // 2048) * 16
        small = jnp.pad(small, (0, rows * 128 - small.shape[0])).reshape(rows, 128)
        routed = routed.reshape(-1, 128)
        arrays = [small, w_query, w_keyval, w_out, routed, w_latent.T, cotangent]
        plans = [
            (a, "yz" if a == 3 else "zy", v.shape[0], v.shape[0], 0, "", 0, 0)
            for a, v in enumerate(arrays[:5])
        ]
        quarter = w_latent.shape[1] // n_tensor
        plans.append((5, "zyxc", quarter, quarter, 0, "xc", quarter, 0))
        block, half_rows = rows_part // 2, n_expert * seq_len // 2
        plans += [
            (6, "zyxc", block, block, h * half_rows, "xc", rows_part, h * block) for h in range(2)
        ]
        small, query_full, keyval_full, outproj_full, routed_all, latent_t, dy_gathered = gather(
            arrays, plans, SIZES, 1
        )
        latent_t = latent_t.reshape(n_expert, -1, w_latent.shape[0])
        latent_t = jnp.swapaxes(latent_t, 0, 1).reshape(-1, D)
        routed_all = routed_all.reshape(n_expert * n_tensor, 2, block, experts_all)
        routed_all = jnp.swapaxes(routed_all, 0, 1).reshape(-1, experts_all)
        routed_all = jnp.pad(routed_all, ((0, 0), (0, 128 - experts_all)))
        shared_gate, shared_up, shared_down, query_full = lax.optimization_barrier(
            (shared_gate, shared_up, shared_down, query_full)
        )
        small = small.reshape(n_expert, rows * 128)
    else:
        small = lax.all_gather(small, "expert", axis=0)
        latent_t = lax.all_gather(w_latent, "expert", axis=0, tiled=True).T
        query_full = lax.all_gather(w_query, "expert", axis=0, tiled=True)
        keyval_full = lax.all_gather(w_keyval, "expert", axis=0, tiled=True)
        outproj_full = lax.all_gather(w_out, "expert", axis=0, tiled=True)
    gain_in_f = small[:, :n_gain].reshape(-1).astype(jnp.float32)
    gain_mid_f = small[:, n_gain : 2 * n_gain].reshape(-1).astype(jnp.float32)
    gain_lat_f = small[:, 2 * n_gain : 2 * n_gain + n_lat].reshape(-1).astype(jnp.float32)
    n_router = w_router.shape[0] * experts_all
    router_full = small[:, 2 * n_gain + n_lat :][:, :n_router].reshape(D, experts_all)
    heads_local = query_full.shape[1] // (NOPE + ROPE)

    sh_here = shared_gate.shape[1] // n_expert
    sh_rows = shared_gate.shape[0]
    units = expert_gate.shape[2]
    lengths = [units] * experts_here + [sh_here]
    shared_w = jnp.stack([shared_gate.T, shared_up.T, shared_down.T])
    shared_w = shared_w.reshape(3, n_expert, sh_here, sh_rows)
    if direct():
        segments_w = [-(-length // 128) * 128 for length in lengths]
        shared_w = jnp.pad(shared_w, ((0, 0), (0, 0), (0, -sh_here % 16), (0, 0)))
    else:
        segments_w = lengths
    shared_w = lax.all_to_all(shared_w, "expert", split_axis=1, concat_axis=0)
    starts = [sum(segments_w[:i]) for i in range(len(lengths))]
    gate_t, up_t = jnp.swapaxes(expert_gate, 1, 2), jnp.swapaxes(expert_up, 1, 2)
    if not direct():
        gate_t, up_t, down_w = [
            jnp.concatenate(
                [v[i] for i in range(experts_here)]
                + [jnp.swapaxes(shared_w[:, which], 0, 1).reshape(sh_here, D)]
            )
            for which, v in enumerate([gate_t, up_t, expert_down])
        ]

    tok_f = tokens.astype(jnp.float32)
    inv_in = inv_rms(tok_f)
    normed = (tok_f * inv_in * gain_in_f).astype(jnp.bfloat16)
    query_lin = dot_plain(normed, query_full).reshape(seq_len, heads_local, NOPE + ROPE)
    seg_ids = segments[0]
    cos_tab, sin_tab = rope_tables(doc_positions(seg_ids))
    q_nope = query_lin[..., :NOPE].astype(jnp.bfloat16)
    q_rope = rotate(query_lin[..., NOPE:], cos_tab[:, None, :], sin_tab[:, None, :]).astype(
        jnp.bfloat16
    )
    latent_all = dot_last(normed, latent_t)
    latent = latent_all[:, :KVR]
    inv_lat = inv_rms(latent)
    latent_n = (latent * inv_lat * gain_lat_f).astype(jnp.bfloat16)
    keyval = dot_plain(latent_n, keyval_full).reshape(seq_len, heads_local, NOPE + VD)
    key_nope = keyval[..., :NOPE].astype(jnp.bfloat16)
    values = keyval[..., NOPE:].astype(jnp.bfloat16)
    key_rope = rotate(latent_all[:, KVR:], cos_tab, sin_tab).astype(jnp.bfloat16)
    scores = masked_scores(q_nope, q_rope, key_nope, key_rope, seg_ids, seg_ids, 0)
    top_val = jnp.max(scores, axis=-1, keepdims=True)
    expo = jnp.exp(scores - top_val)
    probs = expo / jnp.sum(expo, axis=-1, keepdims=True)
    probs_b = probs.astype(jnp.bfloat16)
    attended = jnp.einsum("hqk,khd->qhd", probs_b, values, preferred_element_type=jnp.float32)
    attended = attended.astype(jnp.bfloat16).reshape(seq_len, heads_local * VD)
    attn_rows = scatter_tensor(dot_last(attended, outproj_full).astype(jnp.bfloat16), 2)

    residual = my_rows(tok_f) + attn_rows
    inv_mid = inv_rms(residual)
    normed_mid = (residual * inv_mid * gain_mid_f).astype(jnp.bfloat16)
    def routing(rows_in, mask):
        prob = jax.nn.sigmoid(dot_plain(rows_in, router_full))
        chosen = prob * mask
        chosen_sum = jnp.sum(chosen, axis=1, keepdims=True)
        return prob, chosen_sum, ROUTE_SCALE * chosen / chosen_sum

    routed_units = experts_here * units

    def mixture(normed_part, dy_part, route_part):
        normed_all = lax.all_gather(normed_part, both, axis=0, tiled=True)
        dy_all = lax.all_gather(dy_part, both, axis=0, tiled=True)
        mask_all = lax.all_gather(route_part, both, axis=0, tiled=True).astype(jnp.float32)
        n_all = normed_all.shape[0]
        weights_here = lax.dynamic_slice_in_dim(
            routing(normed_all, mask_all)[2], expert_pos * experts_here, experts_here, 1
        )
        scale = jnp.concatenate(
            [jnp.broadcast_to(weights_here[:, i : i + 1], (n_all, units)) for i in range(experts_here)]
            + [jnp.ones((n_all, sh_here), jnp.float32)],
            axis=1,
        )
        gate_x = dot_last(normed_all, gate_t)
        up_x = dot_last(normed_all, up_t)
        grad_h = dot_last(dy_all, down_w)
        sig_x = jax.nn.sigmoid(gate_x)
        silu_x = gate_x * sig_x
        hidden = silu_x * up_x
        hidden_s = (hidden * scale).astype(jnp.bfloat16)
        grad_gates = (grad_h * hidden)[:, :routed_units]
        grad_gates = jnp.sum(grad_gates.reshape(n_all, experts_here, units), axis=2)
        grad_hs = grad_h * scale
        grad_gate_x = (grad_hs * up_x * sig_x * (1.0 + gate_x * (1.0 - sig_x))).astype(jnp.bfloat16)
        grad_up_x = (grad_hs * silu_x).astype(jnp.bfloat16)
        out_x = dot_plain(hidden_s, down_w).astype(jnp.bfloat16)
        grad_x = (dot_plain(grad_gate_x, gate_t) + dot_plain(grad_up_x, up_t)).astype(jnp.bfloat16)
        grad_gates = lax.dynamic_update_slice_in_dim(
            jnp.zeros((n_all, experts_all), jnp.float32), grad_gates, expert_pos * experts_here, 1
        )
        grad_rows = lax.psum_scatter(grad_x, both, scatter_dimension=0, tiled=True)
        grad_gates = lax.psum_scatter(grad_gates, both, scatter_dimension=0, tiled=True)
        moe_rows = lax.psum_scatter(out_x, both, scatter_dimension=0, tiled=True)
        return (moe_rows, grad_rows, grad_gates), (
            dot_first(grad_gate_x, normed_all),
            dot_first(grad_up_x, normed_all),
            dot_first(hidden_s, dy_all),
        )

    inputs = (normed_mid, my_rows(cotangent), my_routed)
    pieces = max(1, n_expert * seq_len // 4096)
    if direct():
        router_w = jnp.pad(router_full, ((0, 0), (0, 128 - experts_all)))
        weights_w = (gate_t, up_t, expert_down, shared_w)
        x_all, hidden_s, grad_gate_up, gate_sums = mixture_forward(
            normed_mid, dy_gathered, routed_all, weights_w, router_w, segments_w, 3
        )
        sums, out_x, unit_rows = mixture_backward(
            hidden_s, grad_gate_up, gate_sums, residual, weights_w, segments_w, 5
        )
        sums, out_x = lax.optimization_barrier((sums, out_x))
        out_x = out_x.reshape(n_expert * n_tensor * seq_len, D // n_tensor)
        moe_rows = lax.psum_scatter(out_x, both, scatter_dimension=0, tiled=True)
        by_row = (moe_rows, sums[:, :D], sums[:, D : D + experts_all])
    elif pieces == 1:
        by_row, by_weight = mixture(*inputs)
    else:
        inputs = [v.reshape(pieces, rows_part // pieces, v.shape[1]) for v in inputs]
        total = tuple(jnp.zeros(gate_t.shape, jnp.float32) for _ in range(3))

        def one_piece(total, piece):
            rows_out, more = mixture(*piece)
            return tuple(a + b for a, b in zip(total, more)), rows_out

        by_weight, by_row = lax.scan(one_piece, total, inputs)
        by_row = tuple(v.reshape(rows_part, v.shape[2]) for v in by_row)
    moe_rows, grad_mid, grad_gates = by_row
    moe_rows, grad_mid = moe_rows.astype(jnp.float32), grad_mid.astype(jnp.float32)
    mask = my_routed.astype(jnp.float32)
    prob, chosen_sum, weights = routing(normed_mid, mask)
    grad_prob = (
        mask
        * (ROUTE_SCALE * grad_gates - jnp.sum(grad_gates * weights, axis=1, keepdims=True))
        / chosen_sum
    )
    grad_logit = grad_prob * prob * (1.0 - prob)
    grad_mid = grad_mid + jnp.dot(grad_logit, router_full.astype(jnp.float32).T, precision=HIGH)
    grad_router = jnp.dot(normed_mid.astype(jnp.float32).T, grad_logit, precision=HIGH)
    resid_part, grad_gain_mid = norm_back(residual, inv_mid, gain_mid_f, grad_mid)
    grad_resid = my_rows(cotangent).astype(jnp.float32) + resid_part
    grad_attn = gather_tensor(grad_resid.astype(jnp.bfloat16), 6)

    grad_outproj = dot_first(grad_attn, attended)
    grad_att = (
        dot_plain(grad_attn, outproj_full).astype(jnp.bfloat16).reshape(seq_len, heads_local, VD)
    )
    score_scale = (NOPE + ROPE) ** (-0.5)
    grad_probs = jnp.einsum("qhd,khd->hqk", grad_att, values, preferred_element_type=jnp.float32)
    delta_sum = jnp.sum(probs * grad_probs, axis=-1, keepdims=True)
    grad_scores = (probs * (grad_probs - delta_sum)).astype(jnp.bfloat16)
    grad_qn = (
        jnp.einsum("hqk,khd->qhd", grad_scores, key_nope, preferred_element_type=jnp.float32)
        * score_scale
    )
    grad_qr = (
        jnp.einsum("hqk,kd->qhd", grad_scores, key_rope, preferred_element_type=jnp.float32)
        * score_scale
    )
    grad_knope = (
        jnp.einsum("hqk,qhd->khd", grad_scores, q_nope, preferred_element_type=jnp.float32)
        * score_scale
    )
    grad_krope = (
        jnp.einsum("hqk,qhd->kd", grad_scores, q_rope, preferred_element_type=jnp.float32)
        * score_scale
    )
    grad_values = jnp.einsum(
        "hqk,qhd->khd", probs_b, grad_att, preferred_element_type=jnp.float32
    )
    grad_qr = unrotate(grad_qr, cos_tab[:, None, :], sin_tab[:, None, :])
    grad_query = (
        jnp.concatenate([grad_qn, grad_qr], axis=-1)
        .reshape(seq_len, heads_local * (NOPE + ROPE))
        .astype(jnp.bfloat16)
    )
    grad_wquery = dot_first(normed, grad_query)
    grad_normed = dot_last(grad_query, query_full)
    grad_keyval = (
        jnp.concatenate([grad_knope, grad_values], axis=-1)
        .reshape(seq_len, heads_local * (NOPE + VD))
        .astype(jnp.bfloat16)
    )
    grad_wkeyval = dot_first(latent_n, grad_keyval)
    grad_latent_n = dot_last(grad_keyval, keyval_full)
    grad_latent, grad_gain_lat = norm_back(latent, inv_lat, gain_lat_f, grad_latent_n)
    grad_latent_all = jnp.concatenate(
        [grad_latent, unrotate(grad_krope, cos_tab, sin_tab)], axis=-1
    )
    grad_latent_all = grad_latent_all.astype(jnp.bfloat16)
    grad_normed = grad_normed + dot_plain(grad_latent_all, latent_t)
    n_latent = w_latent.shape[1]
    if direct():
        grad_latent_all = jnp.pad(grad_latent_all, ((0, 0), (0, -n_latent % 128)))
    grad_wlatent = dot_first(normed, grad_latent_all)
    tok_part, grad_gain_in = norm_back(tok_f, inv_in, gain_in_f, grad_normed)

    n_dev = n_expert * n_tensor
    shared_small = [grad_gain_in, grad_gain_mid, grad_gain_lat, grad_router]
    shared_small = jnp.concatenate([v.reshape(n_dev, -1) for v in shared_small], axis=1)
    parts = [grad_wquery, grad_wkeyval, grad_outproj, grad_wlatent, shared_small, tok_part]
    parts = [v.astype(jnp.bfloat16) for v in parts]
    if direct():
        n_small = parts[4].shape[1]
        rows = -(-n_small // 2048) * 16
        parts[4] = jnp.pad(parts[4], ((0, 0), (0, rows * 128 - n_small))).reshape(-1, 128)
        orders = ["zy", "zy", "yz", "zyxc", "zyxc", "xc"]
        counts = [n_expert, n_expert, n_expert, n_dev, n_dev, n_tensor]
        plans = [
            (a, orders[a], v.shape[0] // counts[a], v.shape[0] // counts[a], 0)
            for a, v in enumerate(parts)
        ]
        a, order, rows, pitch, _ = plans[2]
        plans[2] = (a, order, rows // 2, pitch, 0)
        plans.append((a, order[::-1], rows // 2, pitch, rows // 2))
        (
            out_wquery, out_wkeyval, out_wout, out_wlatent, shared_small, tok_sum,
            out_egate, out_eup, out_edown, *shared_g,
        ) = final_sums(
            parts, plans, unit_rows, x_all, dy_gathered, segments_w, experts_here, units, sh_here, 7,
        )
        shared_small = shared_small.reshape(-1)[:n_small]
    else:
        axes = ["expert", "expert", "expert", both, both, "tensor"]
        out_wquery, out_wkeyval, out_wout, out_wlatent, shared_small, tok_sum = [
            lax.psum_scatter(v, axis, scatter_dimension=0, tiled=True).astype(jnp.float32)
            for v, axis in zip(parts, axes)
        ]
        shared_small = shared_small[0]
        out_egate, out_eup, out_edown = [
            jnp.stack([v[at : at + units] for at in starts[:-1]]) for v in by_weight
        ]
        shared_g = jnp.stack([v[starts[-1] : starts[-1] + sh_here] for v in by_weight])
        shared_g = shared_g.astype(jnp.bfloat16).reshape(3, sh_here, n_expert, sh_rows)
        shared_g = lax.all_to_all(shared_g, "expert", split_axis=2, concat_axis=1)
        shared_g = shared_g.reshape(3, n_expert * sh_here, sh_rows).astype(jnp.float32)
    out_egate, out_eup = jnp.swapaxes(out_egate, 1, 2), jnp.swapaxes(out_eup, 1, 2)
    tok_sum, moe_rows = lax.optimization_barrier((tok_sum, moe_rows))
    if direct():
        mixed = moe_rows.astype(jnp.bfloat16)
    else:
        mixed = (residual + moe_rows).astype(jnp.bfloat16)
        mixed = lax.all_to_all(
            mixed.reshape(rows_part, n_tensor, D // n_tensor), "tensor", split_axis=1, concat_axis=0
        ).reshape(seq_len, D // n_tensor)
    tokens_grad = (tok_sum + grad_resid).astype(jnp.bfloat16)
    n_gain, n_lat = D // n_dev, KVR // n_dev
    cuts = [n_gain, 2 * n_gain, 2 * n_gain + n_lat]
    out_gain_in, out_gain_mid, out_gain_lat, out_router = jnp.split(shared_small, cuts)
    return (
        mixed,
        tokens_grad,
        out_gain_in,
        out_wquery,
        out_wlatent[:, :n_latent],
        out_gain_lat,
        out_wkeyval,
        out_wout,
        out_gain_mid,
        out_router.reshape(D // n_dev, experts_all),
        shared_g[0].T,
        shared_g[1].T,
        shared_g[2].T,
        out_egate,
        out_eup,
        out_edown,
    )


def solution(mesh):
    in_specs = (
        P("expert", None),
        P("expert", None),
        P("expert", None),
        P("expert", None),
        P("expert"),
        P("expert", "tensor"),
        P("expert", None),
        P("expert"),
        P("expert", "tensor"),
        P("expert", "tensor"),
        P("expert"),
        P("expert", None),
        P("expert", "tensor"),
        P("expert", "tensor"),
        P("expert", "tensor"),
        P("expert", None, "tensor"),
        P("expert", None, "tensor"),
        P("expert", "tensor", None),
    )
    out_specs = (
        P("expert", "tensor"),
        P(("expert", "tensor"), None),
        P(("expert", "tensor")),
        P("expert", "tensor"),
        P(("expert", "tensor"), None),
        P(("expert", "tensor")),
        P("expert", "tensor"),
        P("expert", "tensor"),
        P(("expert", "tensor")),
        P(("expert", "tensor"), None),
        P("expert", "tensor"),
        P("expert", "tensor"),
        P("expert", "tensor"),
        P("expert", None, "tensor"),
        P("expert", None, "tensor"),
        P("expert", "tensor", None),
    )
    return jax.shard_map(local, mesh=mesh, in_specs=in_specs, out_specs=out_specs, check_vma=False)
```

time: 3430 us -> 714 us (0.21)
  blocking collectives: 1420 us -> 0 us
  waiting for transfers between devices: 1260 us -> 0.02 us
  Pallas kernels: 0 us -> 535 us
  local copies, waits for them, and re-layouts: 300 us -> 51.5 us
  matrix products: 295 us -> 64.1 us
  other arithmetic: 99.2 us -> 32 us
    all_to_all x2 -> x0, blocking collectives: 909 us -> none  [send_rows(): lax.all_to_all(rows_in, 'expert', split_axis=0, concat_axis=0, tiled=True)]
    all_gather x7 -> x0, waiting for transfers between devices: 706 us -> none  [the longest x1 383 us: local(): lax.all_gather(shared_up, 'expert', axis=0, tiled=True)]
    pallas_call x0 -> x6, Pallas kernels: none -> 535 us  [the longest x2 168 us: gather(): pl.pallas_call(kernel, out_shape=shapes, in_specs=[pl.BlockSpec(memory_sp...]
    reduce_scatter x10 -> x1, waiting for transfers between devices: 466 us -> 0.01 us  [local(): moe_rows = lax.psum_scatter(out_x, both, scatter_dimension=0, tiled=True)]
    all_gather x3 -> x0, blocking collectives: 461 us -> none  [the longest x1 426 us: local(): lax.all_gather(w_router, 'expert', axis=0, tiled=True)]
    dot_general x21 -> x8, matrix products: 212 us -> 17.9 us  [the longest x1 5.72 us: local(): jnp.einsum('hqk,qhd->khd', probs_b, grad_att, preferred_element_type=jnp....]
    gather x4 -> x0, local copies, waits for them, and re-layouts: 149 us -> none  [the longest x1 41.3 us: local(): grad_out[source_tok] * gate_slots[:, None]]
    convert_element_type x3 -> x4, local copies, waits for them, and re-layouts: 57.4 us -> 1.04 us  [the longest x2 0.87 us: local(): jnp.any(routes[:, :, None] == expert_ids[None, None, :], axis=1)]
  transfers between devices with their start and end apart: 23 -> 2, of which waited for: 18 -> 0; matrix products, arithmetic and copies ran while one was open for 8% -> 17% of each run, Pallas kernels for 0% -> 28%
where the time goes in v1:
time: 714 us; the launch traced here: 702 us
  Pallas kernels  535 us (75%)
  matrix products  64.1 us (9%)
  local copies, waits for them, and re-layouts  51.5 us (7%)
  other arithmetic  32 us (4%)
  between operations  15.2 us (2%)
    pallas_call x2, Pallas kernels, gather(): pl.pallas_call(kernel, out_shape=shapes, in_specs=[pl.BlockSpec(memory_sp...  168 us
    pallas_call x1, Pallas kernels, final_sums(): pl.pallas_call(kernel, out_shape=shapes, in_specs=[any_spec] * (n_arrays...  151 us
    pallas_call x1, Pallas kernels, mixture_forward(): pl.pallas_call(kernel, out_shape=[jax.ShapeDtypeStruct((n_rows, width), b...  108 us
    pallas_call x1, Pallas kernels, mixture_backward(): pl.pallas_call(kernel, out_shape=[jax.ShapeDtypeStruct((2 * block, all_wi...  92.1 us
    unnamed x180, local copies, waits for them, and re-layouts  28.2 us
    pallas_call x1, Pallas kernels, scatter(): pl.pallas_call(kernel, out_shape=shapes, in_specs=[pl.BlockSpec(memory_sp...  16.5 us
    dot_general x5, matrix products, dot_plain(): return jnp.dot(left_m, right_m, preferred_element_type=jnp.float32)  15.8 us
  transfers between devices with their start and end apart: 2, of which 0 were waited for; matrix products, arithmetic and copies ran while one was open for 17% of the time, Pallas kernels for 28%

profile of v1, /device:TPU:0, one launch (start us, length us, event | category | flops | bytes accessed | tf_op | source)
XLA Modules:
  0.0 701.6 jit_solution(7993544138287495953)
XLA Ops:
  12.6 139.8 %shard_map.297 = (bf16[384,128]{1,0:T(8,128)(2,1)}, bf16[2048,768]{1,0:T(8,128)(2,1)}, bf16[512,1024]{1,0:T(8,128)(2,1)}, bf16[2048,512]{1,0:T(8,128)(2,1)}, bf1...) custom-call(bf16[48,128]{1,0:T(8,128)(2,1)} %pad_bitcast_fusion.refs_0_, ...), custom_call_target="tpu_custom_call" | custom-call | tf_op jit(solution)/shard_map/pallas_call | solution.py:273
  153.6 3.7 all-to-all-start
  158.0 3.5 copy.153
  162.7 3.2 fusion.62
  168.8 3.1 reshape.352
  171.9 2.5 fusion.65
  174.5 5.0 fusion.60
  186.2 3.1 fusion.11
  189.3 2.5 convert_element_type.142
  193.3 6.3 fusion.67
  199.6 4.6 convolution_convert_fusion.9
  204.2 4.4 convolution_convert_fusion.3.refs_0_
  208.7 16.5 %shard_map.298 = f32[128,2048]{1,0:T(8,128)} custom-call(bf16[512,2048]{1,0:T(8,128)(2,1)} %convolution_convert_fusion.3.refs_0_), custom_call_target="tpu_custom_call" | custom-call | tf_op jit(solution)/shard_map/pallas_call | solution.py:384
  233.8 107.6 %shard_map.299 = (bf16[4096,2048]{1,0:T(8,128)(2,1)}, bf16[4096,896]{1,0:T(8,128)(2,1)}, bf16[4096,1792]{1,0:T(8,128)(2,1)}, bf16[4096,128]{1,0:T(8,128)(2,1)}) custom-call(bf16[128,2048]{1,0:T(8,128)(2,1)} %multiply_convert_fusion.1.nm, bf16[4096,2048]{1,0:T(8,128)(2,1)} %get-tuple-element.56.dy.refs_8_, bf16[4096,128]{1,0:T(8,128)(2,1)} %pad.25.mask, ...), custom_call_target="tpu_custom_call" | custom-call | tf_op jit(solution)/shard_map/pallas_call | solution.py:727
  341.5 92.1 %shard_map.300 = (f32[128,2176]{1,0:T(8,128)}, bf16[8,4,4,2,64,512]{5,4,3,2,1,0:T(8,128)(2,1)}, bf16[2688,4096]{1,0:T(8,128)(2,1)}) custom-call(bf16[4096,896]{1,0:T(8,128)(2,1)} %get-tuple-element.61.hid_in, bf16[4096,1792]{1,0:T(8,128)(2,1)} %get-tuple-element.62.dgu_in, bf16[4096,128]{1,0:T(8,128)(2,1)} %get-tuple-element.63.gg_in, f32[128,2048]{1,0:T(8,128)} %copy-done, ...), custom_call_target="tpu_custom_call" | custom-call | tf_op jit(solution)/shard_map/pallas_call | solution.py:915
  436.0 2.8 multiply_reduce_fusion.2
  438.8 2.6 fusion.64
  441.4 27.8 %shard_map.301 = bf16[512,2048]{1,0:T(8,128)(2,1)} custom-call(bf16[128,2048]{1,0:T(8,128)(2,1)} %get-tuple-element.154.refs_0_), custom_call_target="tpu_custom_call" | custom-call | tf_op jit(solution)/shard_map/pallas_call | solution.py:273
  469.2 3.0 convolution_convert_fusion.7
  476.9 5.7 fusion.19
  482.6 2.2 fusion.17
  491.0 5.6 fusion.9
  505.3 3.0 convolution_convert_fusion.5.refs_1_
  508.3 2.7 convolution_convert_fusion.2.refs_2_
  510.9 3.5 convolution_convert_fusion.1.refs_3_
  514.5 3.7 convolution_convert_fusion.refs_0_
  518.2 2.3 fusion.8.refs_5_
  520.5 151.2 %shard_map.302 = (f32[256,768]{1,0:T(8,128)}, f32[64,1024]{1,0:T(8,128)}, f32[256,512]{1,0:T(8,128)}, f32[64,640]{1,0:T(8,128)}, f32[16,128]{1,0:T(8,128)}, /*in...) custom-call(bf16[2048,768]{1,0:T(8,128)(2,1)} %convolution_convert_f, ...), custom_call_target="tpu_custom_call" | custom-call | tf_op jit(solution)/shard_map/pallas_call | solution.py:1188
  675.9 2.2 add_convert_fusion
  683.7 2.9 copy.177
  688.5 2.8 copy.178
  692.0 2.5 copy.179
  (252 shorter events, 61.8 us)
Async XLA Ops:
  7.2 145.2 %copy-start.35 = (bf16[256,704]{0,1:T(8,128)(2,1)S(1)}, bf16[256,704]{0,1:T(8,128)(2,1)}, u32[]{:S(2)}) copy-start(bf16[256,704]{0,1:T(8,128)(2,1)} %param.30) | copy-start | bytes 1081348
  7.2 145.2 %copy-start.34 = (bf16[256,704]{0,1:T(8,128)(2,1)S(1)}, bf16[256,704]{0,1:T(8,128)(2,1)}, u32[]{:S(2)}) copy-start(bf16[256,704]{0,1:T(8,128)(2,1)} %param.31) | copy-start | bytes 1081348
  7.2 145.2 %copy-start.33 = (bf16[256,704]{0,1:T(8,128)(2,1)S(1)}, bf16[256,704]{0,1:T(8,128)(2,1)}, u32[]{:S(2)}) copy-start(bf16[256,704]{0,1:T(8,128)(2,1)} %param.32) | copy-start | bytes 1081348
  152.4 4.9 copy-start.46
  153.6 79.2 %all-to-all-start = ((bf16[1,3,8,96,256]{4,3,1,0,2:T(8,128)(2,1)}), bf16[1,3,8,96,256]{4,3,1,0,2:T(8,128)(2,1)S(1)}, u32[]{:S(2)}, u32[]{:S(2)}) async-start(bf16[1,3,8,96,256]{4,3,1,0,2:T(8,128)(2,1)} %fusion.23), calls=%async_computation | async-start | bytes 2359296 | tf_op jit(solution)/shard_map/all_to_all | solution.py:1319
  157.2 518.6 %reduce-scatter.2.cloned.1.call-start = ((), (), s32[]{:S(2)}) async-start(), calls=%async_computation.2 | async-start | bytes 17301504 | tf_op jit(solution)/shard_map/reduce_scatter | solution.py:1421
  157.4 25.8 %copy-start.68 = (f32[32]{0:T(128)}, f32[32]{0:T(128)S(1)}, u32[]{:S(2)}) copy-start(f32[32]{0:T(128)S(1)} %negate_power_fusion) | copy-start | bytes 388
  161.5 12.9 %copy-start.47 = (f32[1,2,8,128]{3,1,2,0:T(2,128)}, f32[1,2,8,128]{3,1,2,0:T(2,128)S(1)}, u32[]{:S(2)}) copy-start(f32[1,2,8,128]{3,1,2,0:T(2,128)S(1)} %copy.152) | copy-start | bytes 24580
  162.6 11.8 %copy-start.60 = (f32[512]{0:T(512)}, f32[512]{0:T(512)S(1)}, u32[]{:S(2)}) copy-start(f32[512]{0:T(512)S(1)} %get-tuple-element.175) | copy-start | bytes 6148
  166.8 5.1 copy-start.52
  174.5 5.0 copy-start.49
  181.1 5.1 copy-start.20
  184.5 4.8 copy-start.27
  184.5 4.8 copy-start.38
  184.5 4.8 copy-start.40
  231.2 110.2 %copy-start = (f32[128,2048]{1,0:T(8,128)}, f32[128,2048]{1,0:T(8,128)S(1)}, u32[]{:S(2)}) copy-start(f32[128,2048]{1,0:T(8,128)S(1)} %get-tuple-element.157.resid) | copy-start | bytes 3145732
  231.8 109.6 %copy-start.66 = (f32[128]{0:T(128)}, f32[128]{0:T(128)S(1)}, u32[]{:S(2)}) copy-start(f32[128]{0:T(128)S(1)} %get-tuple-element.179) | copy-start | bytes 1540
  433.6 5.2 copy-start.72
  435.0 6.5 copy-start.57
  436.0 5.4 copy-start.64
  441.4 27.8 %copy-start.74 = (bf16[2048,512]{1,0:T(8,128)(2,1)S(1)}, bf16[2048,512]{1,0:T(8,128)(2,1)}, u32[]{:S(2)}) copy-start(bf16[2048,512]{1,0:T(8,128)(2,1)} %get-tuple-element.55) | copy-start | bytes 6291460
  491.0 5.7 copy-start.56
  491.0 6.4 copy-start.71
  491.0 7.1 %copy-start.58 = (f32[128]{0:T(128)S(1)}, f32[128]{0:T(128)}, u32[]{:S(2)}) copy-start(f32[128]{0:T(128)} %copy-done.57) | copy-start | bytes 1540
  491.0 7.1 %copy-start.65 = (f32[128]{0:T(128)S(1)}, f32[128]{0:T(128)}, u32[]{:S(2)}) copy-start(f32[128]{0:T(128)} %copy-done.64) | copy-start | bytes 1540
  499.6 5.6 copy-start.70
  520.5 155.4 %copy-start.14 = (f32[128,2048]{1,0:T(8,128)S(1)}, f32[128,2048]{1,0:T(8,128)}, u32[]{:S(2)}) copy-start(f32[128,2048]{1,0:T(8,128)} %get-tuple-element.155) | copy-start | bytes 3145732
  671.7 6.4 copy-start.23
  671.7 7.3 %copy-start.43 = (f32[64,640]{1,0:T(8,128)S(1)}, f32[64,640]{1,0:T(8,128)}, u32[]{:S(2)}) copy-start(f32[64,640]{1,0:T(8,128)} %get-tuple-element.75) | copy-start | bytes 491524
  671.7 7.9 %copy-start.42 = (f32[64,1024]{1,0:T(8,128)S(1)}, f32[64,1024]{1,0:T(8,128)}, u32[]{:S(2)}) copy-start(f32[64,1024]{1,0:T(8,128)} %get-tuple-element.211) | copy-start | bytes 786436
  675.8 5.3 copy-start.26
  683.7 7.5 %slice-start = ((s8[5767168]{0:T(1024)(128)(4,1)}), s8[4194304]{0:T(1024)(128)(4,1)S(1)}, s32[]{:S(2)}) async-start(s8[5767168]{0:T(1024)(128)(4,1)} %bitcast.119), calls=%async_computation.3 | async-start | bytes 8388608
  (52 other events, 128.9 us)
Sparse Core Ops, SparseCore 0:
  433.7 235.1 reduce-scatter.1
